TPU v7x, 32 devices: a whole 2x2x4 slice. The times are simulated.
32 devices in a mesh: dp: 4 (over y, core), expert: 8 (over z, x).
Axes of the slice: x: 2, y: 2, z: 4, core: 2. Of those that a mesh axis runs over, the one named last changes fastest.
Arguments:
- route_experts: int32 [4096, 8], P(('dp', 'expert')), may hold values from 0 to 63, all different within a row; in each aligned block of 128 rows (0 to 127, 128 to 255, ...) at most 18 rows name the same one
- router_gate_weight: float32 [4096, 8], P(('dp', 'expert')), may hold values from 0.02 to 0.3
- forget_mask: int32 [4096], P(('dp', 'expert')), may hold values 0 or 1
- retain_mask: int32 [4096], P(('dp', 'expert')), may hold values 0 or 1
- layer_output: bfloat16 [4096, 3584], P(('dp', 'expert')), may hold values from -6 to 6
- frozen_output: bfloat16 [4096, 3584], P(('dp', 'expert')), may hold values from -6 to 6
- control_vector: float32 [3584], replicated, may hold values from 0.1 to 1
- saved_hidden: bfloat16 [256, 144, 2048], P(('dp', 'expert')), may hold values from -6 to 6
- adapter_in: bfloat16 [2048, 4096], P('dp', 'expert'), may hold values from -0.125 to 0.125
- adapter_out: bfloat16 [3584, 4096], P('dp', 'expert'), may hold values from -0.09375 to 0.09375
Outputs:
- grad_in: float32 [2048, 4096], P('dp', 'expert')
- grad_out: float32 [3584, 4096], P('dp', 'expert')
Inputs may be any that keep to these rules, and one draw needn't show every extreme that they name: `route_experts`: each row names 8 different experts; within the 128 rows of one device no expert is named more than 18 times, a bound that some block reaches.
All inputs are finite; a program needn't handle non-finite values. No bound on the sum of `forget_mask` or of `retain_mask` on one device may be relied on, other than what follows from the above.
Results may differ from a plain program's by a relative error of at most 0.0041.
Values may be sent and summed in bfloat16 or wider, within the bound.
A program may use at most 128 MiB of HBM per device.

v0:
```python
import jax
import jax.numpy as jnp
from jax import lax
from jax.sharding import PartitionSpec as P

steer_coef = 20.0
retain_weight = 1.5
adapter_scale_factor = 2.0
grad_coef = 0.0625


def route_slots(experts_flat, count_all, capacity):
    onehot = (experts_flat[:, None] == jnp.arange(count_all, dtype=jnp.int32)[None, :]).astype(
        jnp.int32
    )
    running = jnp.cumsum(onehot, axis=0) - 1
    within = jnp.sum(onehot * running, axis=1)
    return experts_flat * capacity + within


def token_cotangent(layer_output, frozen_output, forget_mask, retain_mask, control_vector):
    unit = control_vector / jnp.sqrt(jnp.sum(control_vector * control_vector))
    current = layer_output.astype(jnp.float32)
    forget_term = current - steer_coef * unit[None, :]
    retain_term = current - frozen_output.astype(jnp.float32)
    forget_weight = forget_mask.astype(jnp.float32)[:, None]
    retain_part = retain_mask.astype(jnp.float32)[:, None]
    return grad_coef * (forget_weight * forget_term + retain_weight * retain_part * retain_term)


def local(
    route_experts,
    router_gate_weight,
    forget_mask,
    retain_mask,
    layer_output,
    frozen_output,
    control_vector,
    saved_hidden,
    adapter_in,
    adapter_out,
):
    experts_here = saved_hidden.shape[0]
    slot_count = saved_hidden.shape[1]
    hidden_width = saved_hidden.shape[2]
    feature_width = layer_output.shape[1]
    rank_width = adapter_in.shape[1] // experts_here
    expert_devices = lax.axis_size("expert")
    data_devices = lax.axis_size("dp")
    capacity = slot_count // expert_devices
    experts_all = experts_here * expert_devices
    output_gradient = token_cotangent(
        layer_output, frozen_output, forget_mask, retain_mask, control_vector
    )
    value_rows = (
        (router_gate_weight[:, :, None] * adapter_scale_factor * output_gradient[:, None, :])
        .reshape(-1, feature_width)
        .astype(jnp.bfloat16)
    )
    expert_slot_index = route_slots(route_experts.reshape(-1), experts_all, capacity)
    outgoing = (
        jnp.zeros((experts_all * capacity, feature_width), jnp.bfloat16)
        .at[expert_slot_index]
        .set(value_rows)
    )
    outgoing = outgoing.reshape(experts_all, capacity, feature_width)
    segment = lax.all_gather(adapter_in, "dp", axis=0, tiled=True)
    rows_now = segment.shape[0]
    hidden_part = saved_hidden
    factor = segment.reshape(rows_now, experts_here, rank_width)
    codes = jnp.einsum(
        "esf,fer->esr", hidden_part, factor, preferred_element_type=jnp.float32
    ).astype(jnp.bfloat16)
    arrived = lax.all_to_all(outgoing, "expert", split_axis=0, concat_axis=1, tiled=True)
    segment = lax.all_gather(adapter_out, "dp", axis=0, tiled=True)
    rows_now = segment.shape[0]
    arrived_part = arrived
    factor = segment.reshape(rows_now, experts_here, rank_width)
    back = jnp.einsum(
        "esd,der->esr", arrived_part, factor, preferred_element_type=jnp.float32
    ).astype(jnp.bfloat16)
    arrived_part = arrived
    product = jnp.einsum("esd,esr->der", arrived_part, codes, preferred_element_type=jnp.float32)
    grad_out = lax.psum_scatter(
        product.reshape(
            feature_width // data_devices * lax.axis_size("dp"), experts_here * rank_width
        ),
        "dp",
        scatter_dimension=0,
        tiled=True,
    )
    hidden_part = saved_hidden
    product = jnp.einsum("esf,esr->fer", hidden_part, back, preferred_element_type=jnp.float32)
    grad_in = lax.psum_scatter(
        product.reshape(
            hidden_width // data_devices * lax.axis_size("dp"), experts_here * rank_width
        ),
        "dp",
        scatter_dimension=0,
        tiled=True,
    )
    return (grad_in, grad_out)


def solution(mesh):
    return jax.shard_map(
        local,
        mesh=mesh,
        in_specs=(
            P(("dp", "expert"), None),
            P(("dp", "expert"), None),
            P(("dp", "expert")),
            P(("dp", "expert")),
            P(("dp", "expert"), None),
            P(("dp", "expert"), None),
            P(),
            P(("dp", "expert"), None, None),
            P("dp", "expert"),
            P("dp", "expert"),
        ),
        out_specs=(P("dp", "expert"), P("dp", "expert")),
        check_vma=False,
    )
```

profile of v0, /device:TPU:0, one launch (start us, length us, event | category | flops | bytes accessed | tf_op | source)
XLA Modules:
  0.0 455.3 jit_solution(17728430118500422943)
XLA Ops:
  7.2 0.8 copy.15
  8.0 0.1 eq.29
  8.0 0.1 eq.25
  8.1 0.7 broadcast_multiply_fusion.1
  8.9 18.0 %reduce-window.6 = s32[64,8,128]{2,1,0:T(8,128)S(1)} reduce-window(s32[64,8,128]{2,1,0:T(8,128)S(1)} %fusion.22, s32[]{:T(128)} %constant.4.clone.1), window={size=1x1x128 pad=0_0x0_0x127_0}, to_apply=%region_0.0 | reduce-window | flops 8323072 | bytes 524292 | tf_op jit(solution)/shard_map/reduce-window
  26.9 0.1 slice.8
  27.0 0.1 copy.17
  27.2 0.1 copy.18
  27.3 0.1 add_add_fusion
  27.4 0.1 copy.14
  27.5 0.1 mul.85
  27.6 1.3 multiply_reduce_fusion
  29.6 0.7 divide_multiply_fusion
  30.4 0.7 convert_element_type.27
  31.0 0.7 convert_multiply_fusion
  31.7 0.7 broadcast_multiply_fusion
  32.4 0.1 copy.19
  32.5 0.1 mul.89
  32.6 0.1 fusion.21
  32.6 2.0 fusion.12
  34.6 15.1 %scatter_custom_fusion = bf16[1152,3584]{1,0:T(8,128)(2,1)} fusion(s32[1024]{0:T(1024)S(1)} %bitcast.46, f32[128,3584]{1,0:T(8,128)S(1)} %fusion.12, f32[1024]{0:T(1024)S(1)} %mul.89, bf16[]{:T(256)} %constant.10.clone.1), kind=kCustom, calls=%fused_computation.3 | custom fusion | flops 7340032 | bytes 10096642 | tf_op jit(solution)/shard_map/scatter | solution.py:64
  49.7 13.2 %reshape.80 = bf16[64,18,3584]{2,1,0:T(8,128)(2,1)} reshape(bf16[1152,3584]{1,0:T(8,128)(2,1)} %scatter_custom_fusion) | data formatting | bytes 16515072 | tf_op jit(solution)/shard_map/reshape | solution.py:66
  62.9 0.0 copy-start
  62.9 0.0 copy-start.1
  62.9 7.4 %all-to-all-start = ((bf16[64,18,3584]{2,1,0:T(8,128)(2,1)}), bf16[64,18,3584]{2,1,0:T(8,128)(2,1)}, u32[]{:S(2)}, u32[]{:S(2)}) async-start(bf16[64,18,3584]{2,1,0:T(8,128)(2,1)} %reshape.80), calls=%async_computation | async-start | bytes 22020096 | tf_op jit(solution)/shard_map/all_to_all | solution.py:74
  70.2 0.0 all-gather.3.cloned.1.call-start
  70.3 0.0 copy-done
  70.3 1.3 copy.22
  71.6 0.0 all-gather.3.cloned.1.call-update
  71.6 0.0 all-gather.5.cloned.1.call-start
  71.7 0.0 copy-done.1
  71.7 1.0 copy.24
  72.7 0.0 all-gather.5.cloned.1.call-update
  72.7 0.2 reduce-scatter.3.cloned.1.call-start
  72.9 236.7 %all-to-all-done = bf16[64,18,3584]{2,1,0:T(8,128)(2,1)} async-done(((bf16[64,18,3584]{2,1,0:T(8,128)(2,1)}), bf16[64,18,3584]{2,1,0:T(8,128)(2,1)}, u32[]{:S(2)}, u32[]{:S(2)}) %all-to-all-start) | async-done | bytes 8257568 | tf_op jit(solution)/shard_map/all_to_all | solution.py:74
  309.6 10.2 %copy.21 = bf16[8,8,18,3584]{3,0,2,1:T(8,128)(2,1)} copy(bf16[8,8,18,3584]{3,2,0,1:T(8,128)(2,1)} %bitcast.7) | data formatting | bytes 16515072 | tf_op jit(solution)/shard_map/all_to_all | solution.py:74
  319.8 0.0 all-gather.3.cloned.1.call-done
  319.8 11.3 %fusion.18 = f32[8,64,2048]{2,1,0:T(8,128)} fusion(bf16[8,144,2048]{2,1,0:T(8,128)(2,1)} %param.17, bf16[3584,8,64]{0,2,1:T(8,128)(2,1)} %bitcast.41, bf16[8,144,3584]{2,0,1:T(8,128)(2,1)} %bitcast.37), kind=kOutput, calls=%fused_computation.19 | convolution fusion | flops 830545920 | bytes 20840448 | tf_op jit(solution)/shard_map/esf,esr->fer/dot_general | solution.py:93
  331.1 5.4 %copy.23 = f32[2048,512]{1,0:T(8,128)} copy(f32[2048,512]{0,1:T(8,128)} %bitcast.40) | data formatting | bytes 8388608 | tf_op jit(solution)/shard_map/reshape | solution.py:95
  336.4 0.0 reduce-scatter.3.cloned.1.call-update
  336.4 0.3 reduce-scatter.5.cloned.1.call-start
  336.7 0.0 all-gather.5.cloned.1.call-done
  336.7 15.9 %fusion.7 = f32[8,64,3584]{2,1,0:T(8,128)} fusion(bf16[8,144,3584]{2,0,1:T(8,128)(2,1)} %bitcast.38, bf16[8,144,2048]{2,1,0:T(8,128)(2,1)} %param.17, bf16[2048,8,64]{0,2,1:T(8,128)(2,1)} %bitcast.42), kind=kOutput, calls=%fused_computation.8 | convolution fusion | flops 830545920 | bytes 22413312 | tf_op jit(solution)/shard_map/esd,esr->der/dot_general | solution.py:83
  352.6 8.5 %copy.26 = f32[3584,512]{1,0:T(8,128)} copy(f32[3584,512]{0,1:T(8,128)} %bitcast.39) | data formatting | bytes 14680064 | tf_op jit(solution)/shard_map/reshape | solution.py:85
  361.1 0.0 reduce-scatter.5.cloned.1.call-update
  361.1 19.1 %reduce-scatter.3.cloned.1.call-done = f32[512,512]{1,0:T(8,128)} async-done(((f32[2048,512]{1,0:T(8,128)}), f32[512,512]{1,0:T(8,128)}) %reduce-scatter.3.cloned.1.call-update) | async-done | bytes 1048592 | tf_op jit(solution)/shard_map/reduce_scatter | solution.py:94
  380.2 68.6 %reduce-scatter.5.cloned.1.call-done = f32[896,512]{1,0:T(8,128)} async-done(((f32[3584,512]{1,0:T(8,128)}), f32[896,512]{1,0:T(8,128)}) %reduce-scatter.5.cloned.1.call-update) | async-done | bytes 1835024 | tf_op jit(solution)/shard_map/reduce_scatter | solution.py:84
  (4 shorter events, 0.1 us)
Async XLA Ops:
  62.9 7.4 %copy-start = (bf16[896,512]{1,0:T(8,128)(2,1)S(1)}, bf16[896,512]{1,0:T(8,128)(2,1)}, u32[]{:S(2)}) copy-start(bf16[896,512]{1,0:T(8,128)(2,1)} %param.19) | copy-start | bytes 2752516
  62.9 8.8 %copy-start.1 = (bf16[512,512]{1,0:T(8,128)(2,1)S(1)}, bf16[512,512]{1,0:T(8,128)(2,1)}, u32[]{:S(2)}) copy-start(bf16[512,512]{1,0:T(8,128)(2,1)} %param.18) | copy-start | bytes 1572868
  62.9 246.7 %all-to-all-start = ((bf16[64,18,3584]{2,1,0:T(8,128)(2,1)}), bf16[64,18,3584]{2,1,0:T(8,128)(2,1)}, u32[]{:S(2)}, u32[]{:S(2)}) async-start(bf16[64,18,3584]{2,1,0:T(8,128)(2,1)} %reshape.80), calls=%async_computation | async-start | bytes 22020096 | tf_op jit(solution)/shard_map/all_to_all | solution.py:74
  70.2 249.5 %all-gather.3.cloned.1.call-start = ((), (), s32[]{:S(2)}) async-start(), calls=%async_computation.3 | async-start | bytes 4587520 | tf_op jit(solution)/shard_map/all_gather | solution.py:75
  71.6 265.1 %all-gather.5.cloned.1.call-start = ((), (), s32[]{:S(2)}) async-start(), calls=%async_computation.5 | async-start | bytes 2621440 | tf_op jit(solution)/shard_map/all_gather | solution.py:67
  72.7 307.5 %reduce-scatter.3.cloned.1.call-start = ((), (), s32[]{:S(2)}) async-start(), calls=%async_computation.4 | async-start | bytes 5242880 | tf_op jit(solution)/shard_map/reduce_scatter | solution.py:94
  336.4 112.4 %reduce-scatter.5.cloned.1.call-start = ((), (), s32[]{:S(2)}) async-start(), calls=%async_computation.6 | async-start | bytes 9175040 | tf_op jit(solution)/shard_map/reduce_scatter | solution.py:84
Sparse Core Ops, SparseCore 0:
  73.2 32.9 all-gather.2
  108.3 22.5 all-gather.4
  336.5 43.5 reduce-scatter.2
  383.3 65.4 reduce-scatter.4
where the time goes:
time: 456 us; the launch traced here: 455 us
  waiting for transfers between devices  324 us (71%)
  local copies, waits for them, and re-layouts  41.2 us (9%)
  other arithmetic  40 us (9%)
  matrix products  27.2 us (6%)
  between operations  14.5 us (3%)
  starting transfers between devices  7.95 us (2%)
    all_to_all x1, waiting for transfers between devices, local(): lax.all_to_all(outgoing, 'expert', split_axis=0, concat_axis=1, tiled=True)  237 us
    reduce_scatter x1, waiting for transfers between devices, local(): lax.psum_scatter(product.reshape(feature_width // data_devices * lax.axis...  68.6 us
    reduce_scatter x1, waiting for transfers between devices, local(): lax.psum_scatter(product.reshape(hidden_width // data_devices * lax.axis_...  19.1 us
    another operation x2, other arithmetic  18 us
    dot_general x1, matrix products, local(): jnp.einsum('esd,esr->der', arrived_part, codes, preferred_element_type=jn...  15.9 us
    scatter x1, other arithmetic, local(): outgoing = jnp.zeros((experts_all * capacity, feature_width), jnp.bfloat1...  15.1 us
    reshape x1, local copies, waits for them, and re-layouts, local(): outgoing = outgoing.reshape(experts_all, capacity, feature_width)  13.2 us
    dot_general x1, matrix products, local(): jnp.einsum('esf,esr->fer', hidden_part, back, preferred_element_type=jnp....  11.3 us
  transfers between devices with their start and end apart: 5, of which 3 were waited for; matrix products, arithmetic and copies ran while one was open for 12% of the time, Pallas kernels for 0%

commit v1 on v0

v1 whole, which is shorter than its diff:
```python
import functools

import jax
import jax.numpy as jnp
from jax import lax
from jax.experimental import pallas as pl
from jax.experimental.pallas import tpu as pltpu
from jax.sharding import PartitionSpec as P

steer_coef = 20.0
retain_weight = 1.5
adapter_scale_factor = 2.0
grad_coef = 0.0625

F32 = jnp.float32
BF16 = jnp.bfloat16


def token_cotangent(layer_output, frozen_output, forget_mask, retain_mask, control_vector):
    unit = control_vector / jnp.sqrt(jnp.sum(control_vector * control_vector))
    current = layer_output.astype(F32)
    forget_term = current - steer_coef * unit[None, :]
    retain_term = current - frozen_output.astype(F32)
    forget_weight = forget_mask.astype(F32)[:, None]
    retain_part = retain_mask.astype(F32)[:, None]
    return grad_coef * (forget_weight * forget_term + retain_weight * retain_part * retain_term)


def expand_gate(gate, experts_here, width):
    rank = width // experts_here
    row = lax.broadcasted_iota(jnp.int32, (experts_here, width), 0)
    column = lax.broadcasted_iota(jnp.int32, (experts_here, width), 1)
    spread = ((column >= row * rank) & (column < (row + 1) * rank)).astype(F32)
    return jnp.dot(gate, spread, precision=lax.Precision.HIGHEST, preferred_element_type=F32)


def block_mask(rows, width, experts_here):
    per_row, per_column = rows // experts_here, width // experts_here
    row = lax.broadcasted_iota(jnp.int32, (rows, width), 0)
    column = lax.broadcasted_iota(jnp.int32, (rows, width), 1)
    mask = jnp.zeros((rows, width), jnp.bool_)
    for e in range(experts_here):
        mask |= (
            (row >= e * per_row)
            & (row < (e + 1) * per_row)
            & (column >= e * per_column)
            & (column < (e + 1) * per_column)
        )
    return mask


def project_kernel(experts_here, cot_ref, out_factor_ref, pick_ref, gate_ref, back_ref):
    data, tokens, depth = cot_ref.shape[1:]
    width = out_factor_ref.shape[1]
    rows = pick_ref.shape[-1]
    rank = width // experts_here
    coded = jnp.dot(
        cot_ref[0].reshape(data * tokens, depth), out_factor_ref[...], preferred_element_type=F32
    )
    mask = block_mask(rows, width, experts_here)
    for p in range(data):
        scaled = coded[p * tokens : (p + 1) * tokens] * expand_gate(
            gate_ref[0, p], experts_here, width
        )
        high = scaled.astype(BF16)
        low = (scaled - high.astype(F32)).astype(BF16)
        pick = pick_ref[0, p]
        dims = (((0,), (0,)), ((), ()))
        chosen = lax.dot_general(pick, high, dims, preferred_element_type=F32)
        chosen += lax.dot_general(pick, low, dims, preferred_element_type=F32)
        chosen = jnp.where(mask, chosen, 0.0)
        total = chosen[:, :rank]
        for e in range(1, experts_here):
            total += chosen[:, e * rank : (e + 1) * rank]
        back_ref[p, 0] = total


def outer_kernel(experts_here, cot_ref, codes_ref, pick_ref, gate_ref, grad_ref):
    data, tokens, depth = cot_ref.shape[1:]
    width = grad_ref.shape[1]
    rows = pick_ref.shape[-1]
    mask = block_mask(rows, width, experts_here)

    @pl.when(pl.program_id(0) == 0)
    def _():
        grad_ref[...] = jnp.zeros_like(grad_ref)

    parts = []
    for p in range(data):
        codes = codes_ref[p, 0].astype(F32)
        wide = jnp.where(mask, jnp.concatenate([codes] * experts_here, axis=1), 0.0).astype(BF16)
        laid = jnp.dot(pick_ref[0, p], wide, preferred_element_type=F32)
        parts.append((laid * expand_gate(gate_ref[0, p], experts_here, width)).astype(BF16))
    laid = jnp.concatenate(parts, axis=0)
    grad_ref[...] += lax.dot_general(
        cot_ref[0].reshape(data * tokens, depth),
        laid,
        (((0,), (0,)), ((), ())),
        preferred_element_type=F32,
    )


def local(
    route_experts,
    router_gate_weight,
    forget_mask,
    retain_mask,
    layer_output,
    frozen_output,
    control_vector,
    saved_hidden,
    adapter_in,
    adapter_out,
):
    experts_here, slot_count, hidden_width = saved_hidden.shape
    tokens, feature_width = layer_output.shape
    top = route_experts.shape[1]
    width = adapter_in.shape[1]
    rank = width // experts_here
    along = lax.axis_size("expert")
    data = lax.axis_size("dp")
    capacity = slot_count // along
    rows = experts_here * capacity
    depth = feature_width // data

    info = jnp.concatenate([route_experts.astype(F32), router_gate_weight], axis=1)
    info = lax.all_gather(info, ("dp", "expert"), axis=0, tiled=False)
    info = info.reshape(data, along, tokens, 2 * top).transpose(1, 0, 2, 3)
    first = lax.axis_index("expert") * experts_here
    mine = (first + jnp.arange(experts_here, dtype=jnp.int32)).astype(F32)
    named = info[..., :top, None] == mine
    gate = adapter_scale_factor * jnp.sum(
        jnp.where(named, info[..., top:, None], 0.0), axis=3
    )
    member = jnp.any(named, axis=3)
    earlier = jnp.tril(jnp.ones((tokens, tokens), BF16), -1)
    place = jnp.einsum(
        "ut,ipte->ipue", earlier, member.astype(BF16), preferred_element_type=F32
    )
    place = jnp.where(member, place, -1.0)
    pick = (
        (place[..., None] == jnp.arange(capacity, dtype=jnp.int32).astype(F32))
        .astype(BF16)
        .reshape(along, data, tokens, rows)
    )

    cotangent = token_cotangent(
        layer_output, frozen_output, forget_mask, retain_mask, control_vector
    ).astype(BF16)
    cotangent = cotangent.reshape(tokens, data, depth).transpose(1, 0, 2)
    cotangent = lax.all_to_all(cotangent, "dp", split_axis=0, concat_axis=0, tiled=True)
    cotangent = lax.all_gather(cotangent, "expert", axis=0, tiled=False)

    in_factor = lax.all_gather(adapter_in, "dp", axis=0, tiled=True)
    codes = jnp.einsum(
        "esf,fer->esr",
        saved_hidden,
        in_factor.reshape(hidden_width, experts_here, rank),
        preferred_element_type=F32,
    ).astype(BF16)
    codes = codes.reshape(experts_here, along, capacity, rank).transpose(1, 0, 2, 3)
    codes = lax.all_gather(codes.reshape(along, rows, rank), "dp", axis=0, tiled=False)

    cot_spec = pl.BlockSpec((1, data, tokens, depth), lambda i: (i, 0, 0, 0))
    pick_spec = pl.BlockSpec((1, data, tokens, rows), lambda i: (i, 0, 0, 0))
    gate_spec = pl.BlockSpec((1, data, tokens, experts_here), lambda i: (i, 0, 0, 0))
    slot_spec = pl.BlockSpec((data, 1, rows, rank), lambda i: (0, i, 0, 0))
    params = pltpu.CompilerParams(vmem_limit_bytes=40 * 1024 * 1024)
    cost = pl.CostEstimate(
        flops=2 * along * data * tokens * depth * width,
        bytes_accessed=2 * along * data * tokens * depth,
        transcendentals=0,
    )
    back = pl.pallas_call(
        functools.partial(project_kernel, experts_here),
        grid=(along,),
        in_specs=[
            cot_spec,
            pl.BlockSpec((depth, width), lambda i: (0, 0)),
            pick_spec,
            gate_spec,
        ],
        out_specs=slot_spec,
        out_shape=jax.ShapeDtypeStruct((data, along, rows, rank), F32),
        compiler_params=params,
        cost_estimate=cost,
        name="project",
    )(cotangent, adapter_out, pick, gate)
    back = lax.psum_scatter(back, "dp", scatter_dimension=0, tiled=False)
    back = (
        back.astype(BF16)
        .reshape(along, experts_here, capacity, rank)
        .transpose(1, 0, 2, 3)
        .reshape(experts_here, slot_count, rank)
    )
    grad_out = pl.pallas_call(
        functools.partial(outer_kernel, experts_here),
        grid=(along,),
        in_specs=[cot_spec, slot_spec, pick_spec, gate_spec],
        out_specs=pl.BlockSpec((depth, width), lambda i: (0, 0)),
        out_shape=jax.ShapeDtypeStruct((depth, width), F32),
        compiler_params=params,
        cost_estimate=cost,
        name="outer",
    )(cotangent, codes, pick, gate)
    product = jnp.einsum("esf,esr->fer", saved_hidden, back, preferred_element_type=F32)
    grad_in = lax.psum_scatter(
        product.reshape(hidden_width, width), "dp", scatter_dimension=0, tiled=True
    )
    return (grad_in, grad_out)


def solution(mesh):
    return jax.shard_map(
        local,
        mesh=mesh,
        in_specs=(
            P(("dp", "expert"), None),
            P(("dp", "expert"), None),
            P(("dp", "expert")),
            P(("dp", "expert")),
            P(("dp", "expert"), None),
            P(("dp", "expert"), None),
            P(),
            P(("dp", "expert"), None, None),
            P("dp", "expert"),
            P("dp", "expert"),
        ),
        out_specs=(P("dp", "expert"), P("dp", "expert")),
        check_vma=False,
    )
```

time: 456 us -> 283 us (0.62)
  waiting for transfers between devices: 324 us -> 82.8 us
  blocking collectives: 0 us -> 98.6 us
  Pallas kernels: 0 us -> 35.6 us
  other arithmetic: 40 us -> 10.3 us
  matrix products: 27.2 us -> 10.2 us
  local copies, waits for them, and re-layouts: 41.2 us -> 30.2 us
  starting transfers between devices: 7.95 us -> 0.16 us
    all_to_all x1 -> x0, waiting for transfers between devices: 237 us -> none  [local(): lax.all_to_all(outgoing, 'expert', split_axis=0, concat_axis=1, tiled=True)]
    all_gather x0 -> x2, blocking collectives: none -> 81.5 us  [the longest x1 71 us: local(): info = lax.all_gather(info, ('dp', 'expert'), axis=0, tiled=False)]
    reduce_scatter x2, waiting for transfers between devices: 87.7 us -> 37.3 us  [the longest x1 30.9 us: local(): back = lax.psum_scatter(back, 'dp', scatter_dimension=0, tiled=False)]
    all_gather x2, waiting for transfers between devices: 0.02 us -> 44.7 us  [the longest x1 32.5 us: local(): cotangent = lax.all_gather(cotangent, 'expert', axis=0, tiled=False)]
    pallas_call x0 -> x2, Pallas kernels: none -> 35.6 us  [the longest x1 20.9 us: local(): pl.pallas_call(functools.partial(project_kernel, experts_here), grid=(alo...]
    reshape x3 -> x2, local copies, waits for them, and re-layouts: 27 us -> 5.67 us  [the longest x1 5.51 us: local(): product.reshape(hidden_width, width)]
    another operation x2 -> x0, other arithmetic: 18 us -> none
    all_to_all x0 -> x1, blocking collectives: none -> 17.1 us  [local(): lax.all_to_all(cotangent, 'dp', split_axis=0, concat_axis=0, tiled=True)]
  transfers between devices with their start and end apart: 5 -> 4, of which waited for: 3 -> 4; matrix products, arithmetic and copies ran while one was open for 12% -> 12% of each run, Pallas kernels for 0% -> 5%
where the time goes in v1:
time: 283 us
  blocking collectives  98.6 us (35%)
  waiting for transfers between devices  82.8 us (29%)
  Pallas kernels  35.6 us (13%)
  local copies, waits for them, and re-layouts  30.2 us (11%)
  between operations  14.7 us (5%)
  other arithmetic  10.3 us (4%)
  matrix products  10.2 us (4%)
    all_gather x1, blocking collectives, local(): info = lax.all_gather(info, ('dp', 'expert'), axis=0, tiled=False)  71 us
    all_gather x1, waiting for transfers between devices, local(): cotangent = lax.all_gather(cotangent, 'expert', axis=0, tiled=False)  32.5 us
    reduce_scatter x1, waiting for transfers between devices, local(): back = lax.psum_scatter(back, 'dp', scatter_dimension=0, tiled=False)  30.9 us
    pallas_call x1, Pallas kernels, local(): pl.pallas_call(functools.partial(project_kernel, experts_here), grid=(alo...  20.9 us
    all_to_all x1, blocking collectives, local(): lax.all_to_all(cotangent, 'dp', split_axis=0, concat_axis=0, tiled=True)  17.1 us
    pallas_call x1, Pallas kernels, local(): pl.pallas_call(functools.partial(outer_kernel, experts_here), grid=(along...  14.7 us
    all_gather x1, waiting for transfers between devices, local(): in_factor = lax.all_gather(adapter_in, 'dp', axis=0, tiled=True)  12.3 us
    unnamed x21, local copies, waits for them, and re-layouts  11.3 us
  transfers between devices with their start and end apart: 4, of which 4 were waited for; matrix products, arithmetic and copies ran while one was open for 12% of the time, Pallas kernels for 5%

profile of v1, /device:TPU:0, one launch (start us, length us, event | category | flops | bytes accessed | tf_op | source)
XLA Modules:
  0.0 282.6 jit_solution(16743970534932841865)
XLA Ops:
  7.2 0.0 copy-start.6
  7.2 0.0 all-gather.7.cloned.1.call-start
  7.2 1.4 multiply_reduce_fusion
  9.3 0.7 convert_element_type.47
  10.0 0.7 convert_multiply_fusion
  10.6 0.7 divide_multiply_fusion
  11.4 1.6 copy.78
  12.9 0.0 copy-done.6
  12.9 0.6 copy.79
  13.5 1.6 fusion.3
  15.2 0.0 copy-start.7
  15.2 0.0 copy-start.8
  15.2 17.1 %all_to_all.5 = bf16[4,128,896]{1,2,0:T(8,128)(2,1)S(1)} all-to-all(bf16[4,128,896]{1,2,0:T(8,128)(2,1)S(1)} %bitcast.42), channel_id=1, replica_groups=mesh['dp'=4,'expert'=8] {'dp'}, dimensions={0} | all-to-all | bytes 1835008 | tf_op jit(solution)/shard_map/all_to_all | solution.py:151
  32.3 1.3 copy.80
  33.5 0.0 all-gather.7.cloned.1.call-update
  33.6 0.0 reduce-scatter.3.cloned.1.call-start
  33.6 0.1 eq.39
  33.7 0.0 copy-done.7
  33.7 0.0 copy-done.8
  33.8 71.0 %all-gather.1 = f32[4096,16]{0,1:T(8,128)S(1)} all-gather(f32[128,16]{0,1:T(8,128)S(1)} %pad_maximum_fusion), channel_id=3, replica_groups=mesh['dp'=4,'expert'=8] {'dp','expert'}, dimensions={0}, use_global_device_ids=true | all-gather | bytes 270336 | tf_op jit(solution)/shard_map/all_gather | solution.py:127
  104.8 0.1 copy.95
  104.9 0.2 copy.99
  105.1 0.3 compare_reduce_fusion
  105.3 0.2 fusion.5
  105.6 0.1 copy.82
  105.7 0.2 fusion.6
  105.9 2.0 copy.84
  107.9 0.2 eq.36
  108.0 3.1 %copy.83 = f32[8,4,128,144]{3,2,1,0:T(8,128)} copy(f32[8,4,128,144]{2,0,3,1:T(8,128)S(1)} %bitcast.41) | data formatting | bytes 4718592 | tf_op jit(solution)/shard_map/eq | solution.py:142
  111.2 1.9 broadcast_multiply_fusion.gate_ref
  113.1 0.9 copy-done.5
  114.0 0.0 copy-start.4
  114.0 1.8 compare_convert_fusion.pick_ref
  115.8 32.5 %all-gather.7.cloned.1.call-done = bf16[32,128,896]{2,1,0:T(8,128)(2,1)} async-done(((bf16[4,128,896]{2,1,0:T(8,128)(2,1)}), bf16[32,128,896]{2,1,0:T(8,128)(2,1)}) %all-gather.7.cloned.1.call-update) | async-done | bytes 7340048 | tf_op jit(solution)/shard_map/all_gather | solution.py:152
  148.3 0.0 copy-done.4
  148.3 0.0 copy-start.1
  148.3 1.6 copy-done.1
  149.9 20.9 %project.1 = f32[4,8,144,64]{3,2,1,0:T(8,128)S(1)} custom-call(bf16[8,4,128,896]{3,2,1,0:T(8,128)(2,1)} %bitcast.38, bf16[896,512]{1,0:T(8,128)(2,1)S(1)} %copy-done.4, bf16[8,4,128,144]{3,2,1,0:T(8,128)(2,1)S(1)} %copy-done.1, f32[8,4,128,8]{3,2,1,0:T(8,128)S(1)} %broadcast_multiply_fusion.gate_ref), custom_call_target="tpu_custom_call" | custom-call | flops 3758096384 | bytes 7340032 | tf_op jit(solution)/shard_map/project/pallas_call | solution.py:174
  170.7 0.0 copy-start.3
  170.7 1.5 copy-done.3
  172.2 0.0 reduce-scatter.3.cloned.1.call-update
  172.2 0.0 all-gather.5.cloned.1.call-start
  172.3 0.7 all-gather.5.cloned.1.call-update
  173.0 0.0 reduce-scatter.5.cloned.1.call-start
  173.0 30.9 %reduce-scatter.3.cloned.1.call-done = f32[1,8,144,64]{3,2,1,0:T(8,128)} async-done(((f32[4,8,144,64]{3,2,1,0:T(8,128)}), f32[1,8,144,64]{3,2,1,0:T(8,128)}) %reduce-scatter.3.cloned.1.call-update) | async-done | bytes 294928 | tf_op jit(solution)/shard_map/reduce_scatter | solution.py:189
  203.9 1.1 convert_element_type.56
  205.0 0.1 copy.85
  205.1 0.1 copy.86
  205.2 5.2 %fusion.7 = f32[8,64,2048]{2,1,0:T(8,128)} fusion(bf16[8,144,2048]{2,1,0:T(8,128)(2,1)} %param.17, bf16[8,144,64]{2,0,1:T(8,128)(2,1)S(1)} %bitcast.43), kind=kOutput, calls=%fused_computation.15 | convolution fusion | flops 301989888 | bytes 9060352 | tf_op jit(solution)/shard_map/esf,esr->fer/dot_general | solution.py:206
  210.4 5.5 %copy.88 = f32[2048,512]{1,0:T(8,128)} copy(f32[2048,512]{0,1:T(8,128)} %bitcast.40) | data formatting | bytes 8388608 | tf_op jit(solution)/shard_map/reshape | solution.py:208
  215.9 0.0 reduce-scatter.5.cloned.1.call-update
  215.9 12.3 %all-gather.5.cloned.1.call-done = bf16[2048,512]{1,0:T(8,128)(2,1)} async-done(((bf16[512,512]{1,0:T(8,128)(2,1)}), bf16[2048,512]{1,0:T(8,128)(2,1)}) %all-gather.5.cloned.1.call-update) | async-done | bytes 2097168 | tf_op jit(solution)/shard_map/all_gather | solution.py:154
  228.2 4.0 %copy.89 = bf16[2048,512]{0,1:T(8,128)(2,1)} copy(bf16[2048,512]{1,0:T(8,128)(2,1)} %all-gather.5.cloned.1.call-done) | data formatting | bytes 4194304 | tf_op jit(solution)/shard_map/all_gather | solution.py:154
  232.1 4.7 %convolution_convert_fusion = bf16[8,144,64]{1,2,0:T(8,128)(2,1)S(1)} fusion(bf16[8,144,2048]{2,1,0:T(8,128)(2,1)} %param.17, bf16[2048,8,64]{0,2,1:T(8,128)(2,1)} %bitcast.44), kind=kOutput, calls=%fused_computation.10 | convolution fusion | flops 302063616 | bytes 6963200 | tf_op jit(solution)/shard_map/esf,fer->esr/dot_general | solution.py:155
  236.9 0.2 copy.90
  237.1 0.1 copy.91
  237.2 0.2 copy.92
  237.4 10.5 %all_gather.23 = bf16[4,8,144,64]{2,3,1,0:T(8,128)(2,1)} all-gather(bf16[1,8,144,64]{2,3,1,0:T(8,128)(2,1)S(1)} %copy.92), channel_id=1, replica_groups=mesh['dp'=4,'expert'=8] {'dp'}, dimensions={0}, use_global_device_ids=true | all-gather | bytes 737280 | tf_op jit(solution)/shard_map/all_gather | solution.py:162
  247.9 1.8 copy.93.codes_ref
  249.7 0.0 copy-start
  249.7 3.5 %copy-done = bf16[32,128,896]{2,1,0:T(8,128)(2,1)S(1)} copy-done((bf16[32,128,896]{2,1,0:T(8,128)(2,1)S(1)}, bf16[32,128,896]{2,1,0:T(8,128)(2,1)}, u32[]{:S(2)}) %copy-start) | copy-done | bytes 7340056
  253.2 1.6 copy-done.2
  254.8 14.7 %outer.1 = f32[896,512]{1,0:T(8,128)} custom-call(bf16[8,4,128,896]{3,2,1,0:T(8,128)(2,1)S(1)} %bitcast.39, bf16[4,8,144,64]{3,2,1,0:T(8,128)(2,1)S(1)} %copy.93.codes_ref, bf16[8,4,128,144]{3,2,1,0:T(8,128)(2,1)S(1)} %copy-done.2, f32[8,4,128,8]{3,2,1,0:T(8,128)S(1)} %broadcast_multiply_fusion.gate_ref), custom_call_target="tpu_custom_call" | custom-call | flops 3758096384 | bytes 7340032 | tf_op jit(solution)/shard_map/outer/pallas_call | solution.py:196
  269.5 6.5 %reduce-scatter.5.cloned.1.call-done = f32[512,512]{1,0:T(8,128)} async-done(((f32[2048,512]{1,0:T(8,128)}), f32[512,512]{1,0:T(8,128)}) %reduce-scatter.5.cloned.1.call-update) | async-done | bytes 1048592 | tf_op jit(solution)/shard_map/reduce_scatter | solution.py:207
  (9 shorter events, 0.0 us)
Async XLA Ops:
  7.2 5.8 %copy-start.6 = (bf16[128,3584]{1,0:T(8,128)(2,1)S(1)}, bf16[128,3584]{1,0:T(8,128)(2,1)}, u32[]{:S(2)}) copy-start(bf16[128,3584]{1,0:T(8,128)(2,1)} %param.15) | copy-start | bytes 2752516
  7.2 141.1 %all-gather.7.cloned.1.call-start = ((), (), s32[]{:S(2)}) async-start(), calls=%async_computation.6 | async-start | bytes 8257536 | tf_op jit(solution)/shard_map/all_gather | solution.py:152
  15.2 18.6 %copy-start.7 = (s32[128,8]{0,1:T(8,128)S(1)}, s32[128,8]{0,1:T(8,128)}, u32[]{:S(2)}) copy-start(s32[128,8]{0,1:T(8,128)} %param.10) | copy-start | bytes 12292
  15.2 18.6 %copy-start.8 = (f32[128,8]{0,1:T(8,128)S(1)}, f32[128,8]{0,1:T(8,128)}, u32[]{:S(2)}) copy-start(f32[128,8]{0,1:T(8,128)} %param.11) | copy-start | bytes 12292
  33.6 170.3 %reduce-scatter.3.cloned.1.call-start = ((), (), s32[]{:S(2)}) async-start(), calls=%async_computation.3 | async-start | bytes 2949120 | tf_op jit(solution)/shard_map/reduce_scatter | solution.py:189
  111.2 2.8 copy-start.5
  114.0 34.3 %copy-start.4 = (bf16[896,512]{1,0:T(8,128)(2,1)S(1)}, bf16[896,512]{1,0:T(8,128)(2,1)}, u32[]{:S(2)}) copy-start(bf16[896,512]{1,0:T(8,128)(2,1)} %out_factor_ref.1) | copy-start | bytes 2752516
  148.3 1.6 copy-start.1
  170.7 1.5 copy-start.3
  172.2 55.9 %all-gather.5.cloned.1.call-start = ((), (), s32[]{:S(2)}) async-start(), calls=%async_computation.5 | async-start | bytes 2621440 | tf_op jit(solution)/shard_map/all_gather | solution.py:154
  173.0 103.1 %reduce-scatter.5.cloned.1.call-start = ((), (), s32[]{:S(2)}) async-start(), calls=%async_computation.4 | async-start | bytes 5242880 | tf_op jit(solution)/shard_map/reduce_scatter | solution.py:207
  249.7 3.5 %copy-start = (bf16[32,128,896]{2,1,0:T(8,128)(2,1)S(1)}, bf16[32,128,896]{2,1,0:T(8,128)(2,1)}, u32[]{:S(2)}) copy-start(bf16[32,128,896]{2,1,0:T(8,128)(2,1)} %all-gather.7.cloned.1.call-done) | copy-start | bytes 22020100
  253.2 1.6 copy-start.2
Sparse Core Ops, SparseCore 0:
  33.7 114.5 all-gather.6
  172.4 31.4 reduce-scatter.2
  205.5 22.5 all-gather.4
  231.3 44.7 reduce-scatter.4

commit v2 on v1

--- a/solution.py
+++ b/solution.py
@@ -24,14 +24,6 @@
     forget_weight = forget_mask.astype(F32)[:, None]
     retain_part = retain_mask.astype(F32)[:, None]
     return grad_coef * (forget_weight * forget_term + retain_weight * retain_part * retain_term)
-
-
-def expand_gate(gate, experts_here, width):
-    rank = width // experts_here
-    row = lax.broadcasted_iota(jnp.int32, (experts_here, width), 0)
-    column = lax.broadcasted_iota(jnp.int32, (experts_here, width), 1)
-    spread = ((column >= row * rank) & (column < (row + 1) * rank)).astype(F32)
-    return jnp.dot(gate, spread, precision=lax.Precision.HIGHEST, preferred_element_type=F32)
 
 
 def block_mask(rows, width, experts_here):
@@ -49,7 +41,7 @@
     return mask
 
 
-def project_kernel(experts_here, cot_ref, out_factor_ref, pick_ref, gate_ref, back_ref):
+def project_kernel(experts_here, cot_ref, out_factor_ref, pick_ref, back_ref):
     data, tokens, depth = cot_ref.shape[1:]
     width = out_factor_ref.shape[1]
     rows = pick_ref.shape[-1]
@@ -59,11 +51,9 @@
     )
     mask = block_mask(rows, width, experts_here)
     for p in range(data):
-        scaled = coded[p * tokens : (p + 1) * tokens] * expand_gate(
-            gate_ref[0, p], experts_here, width
-        )
-        high = scaled.astype(BF16)
-        low = (scaled - high.astype(F32)).astype(BF16)
+        own = coded[p * tokens : (p + 1) * tokens]
+        high = own.astype(BF16)
+        low = (own - high.astype(F32)).astype(BF16)
         pick = pick_ref[0, p]
         dims = (((0,), (0,)), ((), ()))
         chosen = lax.dot_general(pick, high, dims, preferred_element_type=F32)
@@ -75,7 +65,7 @@
         back_ref[p, 0] = total
 
 
-def outer_kernel(experts_here, cot_ref, codes_ref, pick_ref, gate_ref, grad_ref):
+def outer_kernel(experts_here, cot_ref, codes_ref, pick_ref, grad_ref):
     data, tokens, depth = cot_ref.shape[1:]
     width = grad_ref.shape[1]
     rows = pick_ref.shape[-1]
@@ -90,7 +80,7 @@
         codes = codes_ref[p, 0].astype(F32)
         wide = jnp.where(mask, jnp.concatenate([codes] * experts_here, axis=1), 0.0).astype(BF16)
         laid = jnp.dot(pick_ref[0, p], wide, preferred_element_type=F32)
-        parts.append((laid * expand_gate(gate_ref[0, p], experts_here, width)).astype(BF16))
+        parts.append(laid.astype(BF16))
     laid = jnp.concatenate(parts, axis=0)
     grad_ref[...] += lax.dot_general(
         cot_ref[0].reshape(data * tokens, depth),
@@ -98,6 +88,20 @@
         (((0,), (0,)), ((), ())),
         preferred_element_type=F32,
     )
+
+
+def sum_over_data(terms, wire):
+    data = terms.shape[0]
+    core = lax.axis_index("dp") % 2
+    pairs = terms.reshape((data // 2, 2) + terms.shape[1:])
+    theirs = lax.dynamic_index_in_dim(pairs, 1 - core, 1, keepdims=False)
+    kept = lax.dynamic_index_in_dim(pairs, core, 1, keepdims=False)
+    kept = kept + lax.ppermute(theirs, "dp", [(i, i ^ 1) for i in range(data)])
+    groups = [list(range(c, data, 2)) for c in range(2)]
+    landed = lax.all_to_all(
+        kept.astype(wire), "dp", split_axis=0, concat_axis=0, axis_index_groups=groups, tiled=True
+    )
+    return jnp.sum(landed.astype(F32), axis=0)
 
 
 def local(
@@ -144,14 +148,24 @@
         .reshape(along, data, tokens, rows)
     )
 
+    slot_gate = jnp.sum(
+        jnp.where(
+            place[..., None] == jnp.arange(capacity, dtype=jnp.int32).astype(F32),
+            gate[..., None],
+            0.0,
+        ),
+        axis=2,
+    ).reshape(along, data, rows, 1)
+
     cotangent = token_cotangent(
         layer_output, frozen_output, forget_mask, retain_mask, control_vector
     ).astype(BF16)
     cotangent = cotangent.reshape(tokens, data, depth).transpose(1, 0, 2)
     cotangent = lax.all_to_all(cotangent, "dp", split_axis=0, concat_axis=0, tiled=True)
+    in_factor = lax.all_gather(adapter_in, "dp", axis=0, tiled=True)
+    cotangent, in_factor = lax.optimization_barrier((cotangent, in_factor))
     cotangent = lax.all_gather(cotangent, "expert", axis=0, tiled=False)
 
-    in_factor = lax.all_gather(adapter_in, "dp", axis=0, tiled=True)
     codes = jnp.einsum(
         "esf,fer->esr",
         saved_hidden,
@@ -160,10 +174,11 @@
     ).astype(BF16)
     codes = codes.reshape(experts_here, along, capacity, rank).transpose(1, 0, 2, 3)
     codes = lax.all_gather(codes.reshape(along, rows, rank), "dp", axis=0, tiled=False)
+    codes = (codes.astype(F32) * slot_gate.transpose(1, 0, 2, 3)).astype(BF16)
+    cotangent, codes = lax.optimization_barrier((cotangent, codes))
 
     cot_spec = pl.BlockSpec((1, data, tokens, depth), lambda i: (i, 0, 0, 0))
     pick_spec = pl.BlockSpec((1, data, tokens, rows), lambda i: (i, 0, 0, 0))
-    gate_spec = pl.BlockSpec((1, data, tokens, experts_here), lambda i: (i, 0, 0, 0))
     slot_spec = pl.BlockSpec((data, 1, rows, rank), lambda i: (0, i, 0, 0))
     params = pltpu.CompilerParams(vmem_limit_bytes=40 * 1024 * 1024)
     cost = pl.CostEstimate(
@@ -178,17 +193,18 @@
             cot_spec,
             pl.BlockSpec((depth, width), lambda i: (0, 0)),
             pick_spec,
-            gate_spec,
         ],
         out_specs=slot_spec,
         out_shape=jax.ShapeDtypeStruct((data, along, rows, rank), F32),
         compiler_params=params,
         cost_estimate=cost,
         name="project",
-    )(cotangent, adapter_out, pick, gate)
-    back = lax.psum_scatter(back, "dp", scatter_dimension=0, tiled=False)
+    )(cotangent, adapter_out, pick)
+    back = sum_over_data(back, F32)
+    own_gate = lax.dynamic_index_in_dim(slot_gate, lax.axis_index("dp"), 1, keepdims=False)
     back = (
-        back.astype(BF16)
+        (back * own_gate)
+        .astype(BF16)
         .reshape(along, experts_here, capacity, rank)
         .transpose(1, 0, 2, 3)
         .reshape(experts_here, slot_count, rank)
@@ -196,17 +212,15 @@
     grad_out = pl.pallas_call(
         functools.partial(outer_kernel, experts_here),
         grid=(along,),
-        in_specs=[cot_spec, slot_spec, pick_spec, gate_spec],
+        in_specs=[cot_spec, slot_spec, pick_spec],
         out_specs=pl.BlockSpec((depth, width), lambda i: (0, 0)),
         out_shape=jax.ShapeDtypeStruct((depth, width), F32),
         compiler_params=params,
         cost_estimate=cost,
         name="outer",
-    )(cotangent, codes, pick, gate)
+    )(cotangent, codes, pick)
     product = jnp.einsum("esf,esr->fer", saved_hidden, back, preferred_element_type=F32)
-    grad_in = lax.psum_scatter(
-        product.reshape(hidden_width, width), "dp", scatter_dimension=0, tiled=True
-    )
+    grad_in = sum_over_data(product.reshape(data, hidden_width // data, width), BF16)
     return (grad_in, grad_out)
 
 

time: 283 us -> 266 us (0.940)
  waiting for transfers between devices: 82.8 us -> 41.2 us
  Pallas kernels: 35.6 us -> 18 us
  local copies, waits for them, and re-layouts: 30.2 us -> 44.2 us
  blocking collectives: 98.6 us -> 109 us
  starting transfers between devices: 0.16 us -> 9.13 us
  other arithmetic: 10.3 us -> 18.6 us
    reduce_scatter x2 -> x0, waiting for transfers between devices: 37.3 us -> none  [the longest x1 30.9 us: local(): back = lax.psum_scatter(back, 'dp', scatter_dimension=0, tiled=False)]
    all_to_all x0 -> x2, waiting for transfers between devices: none -> 16.4 us  [sum_over_data(): lax.all_to_all(kept.astype(wire), 'dp', split_axis=0, concat_axis=0, axis...]
    dynamic_slice x0 -> x6, local copies, waits for them, and re-layouts: none -> 15.7 us  [the longest x3 12.5 us: sum_over_data(): kept = lax.dynamic_index_in_dim(pairs, core, 1, keepdims=False)]
    all_gather x1, waiting for transfers between devices: 32.5 us -> 17.6 us  [local(): cotangent = lax.all_gather(cotangent, 'expert', axis=0, tiled=False)]
    pallas_call x1, Pallas kernels: 20.9 us -> 9.1 us  [local(): pl.pallas_call(functools.partial(project_kernel, experts_here), grid=(alo...]
    all_to_all x1, blocking collectives: 17.1 us -> 26.9 us  [local(): lax.all_to_all(cotangent, 'dp', split_axis=0, concat_axis=0, tiled=True)]
    all_gather x1, waiting for transfers between devices: 12.3 us -> 2.94 us  [local(): in_factor = lax.all_gather(adapter_in, 'dp', axis=0, tiled=True)]
    all_to_all x0 -> x2, starting transfers between devices: none -> 8.97 us  [sum_over_data(): lax.all_to_all(kept.astype(wire), 'dp', split_axis=0, concat_axis=0, axis...]
  transfers between devices with their start and end apart: 4 -> 6, of which waited for: 4 -> 6; matrix products, arithmetic and copies ran while one was open for 12% -> 9% of each run, Pallas kernels for 5% -> 3%
where the time goes in v2:
time: 266 us; the launch traced here: 265 us
  blocking collectives  109 us (41%)
  local copies, waits for them, and re-layouts  44.2 us (17%)
  waiting for transfers between devices  41.2 us (15%)
  other arithmetic  18.6 us (7%)
  Pallas kernels  18 us (7%)
  between operations  15.1 us (6%)
  matrix products  9.54 us (4%)
  starting transfers between devices  9.13 us (3%)
    all_gather x1, blocking collectives, local(): info = lax.all_gather(info, ('dp', 'expert'), axis=0, tiled=False)  71.3 us
    all_to_all x1, blocking collectives, local(): lax.all_to_all(cotangent, 'dp', split_axis=0, concat_axis=0, tiled=True)  26.9 us
    all_gather x1, waiting for transfers between devices, local(): cotangent = lax.all_gather(cotangent, 'expert', axis=0, tiled=False)  17.6 us
    all_to_all x2, waiting for transfers between devices, sum_over_data(): lax.all_to_all(kept.astype(wire), 'dp', split_axis=0, concat_axis=0, axis...  16.4 us
    dynamic_slice x3, local copies, waits for them, and re-layouts, sum_over_data(): kept = lax.dynamic_index_in_dim(pairs, core, 1, keepdims=False)  12.5 us
    unnamed x25, local copies, waits for them, and re-layouts  12.1 us
    all_gather x1, blocking collectives, local(): lax.all_gather(codes.reshape(along, rows, rank), 'dp', axis=0, tiled=False)  10.6 us
    pallas_call x1, Pallas kernels, local(): pl.pallas_call(functools.partial(project_kernel, experts_here), grid=(alo...  9.1 us
  transfers between devices with their start and end apart: 6, of which 6 were waited for; matrix products, arithmetic and copies ran while one was open for 9% of the time, Pallas kernels for 3%

profile of v2, /device:TPU:0, one launch (start us, length us, event | category | flops | bytes accessed | tf_op | source)
XLA Modules:
  0.0 264.5 jit_solution(7483600295067538111)
XLA Ops:
  7.2 0.0 all-gather.5.cloned.1.call-start
  7.2 2.2 copy.78
  9.4 0.0 all-gather.5.cloned.1.call-update
  9.4 0.0 all-gather.7.cloned.1.call-start
  9.5 1.3 multiply_reduce_fusion
  11.5 0.7 convert_element_type.62
  12.2 0.6 copy.76
  12.8 0.6 copy.77
  13.5 1.6 fusion.4
  15.1 26.9 %all_to_all.15 = bf16[4,128,896]{1,2,0:T(8,128)(2,1)S(1)} all-to-all(bf16[4,128,896]{1,2,0:T(8,128)(2,1)S(1)} %bitcast.67), channel_id=1, replica_groups=mesh['dp'=4,'expert'=8] {'dp'}, dimensions={0} | all-to-all | bytes 1835008 | tf_op jit(solution)/shard_map/all_to_all | solution.py:164
  42.0 2.9 %all-gather.5.cloned.1.call-done = bf16[2048,512]{0,1:T(8,128)(2,1)} async-done(((bf16[512,512]{0,1:T(8,128)(2,1)}), bf16[2048,512]{0,1:T(8,128)(2,1)}) %all-gather.5.cloned.1.call-update) | async-done | bytes 2097168 | tf_op jit(solution)/shard_map/all_gather | solution.py:165
  44.9 1.3 copy.79
  46.3 0.1 eq.55
  46.4 71.3 %all-gather.1 = f32[4096,16]{0,1:T(8,128)S(1)} all-gather(f32[128,16]{0,1:T(8,128)S(1)} %pad_maximum_fusion), channel_id=3, replica_groups=mesh['dp'=4,'expert'=8] {'dp','expert'}, dimensions={0}, use_global_device_ids=true | all-gather | bytes 270336 | tf_op jit(solution)/shard_map/all_gather | solution.py:131
  117.7 0.1 copy.104
  117.8 0.2 copy.111
  118.0 0.2 fusion.8
  118.2 0.1 copy.86
  118.3 0.3 compare_reduce_fusion
  118.5 0.2 fusion.7
  118.8 0.1 copy.85
  118.9 0.8 select_reduce_fusion
  119.7 0.3 copy.87
  119.9 0.1 reshape.57
  120.0 0.2 eq.50
  120.2 3.1 %copy.88 = f32[8,4,128,144]{3,2,1,0:T(8,128)} copy(f32[8,4,128,144]{2,0,3,1:T(8,128)S(1)} %bitcast.66) | data formatting | bytes 4718592 | tf_op jit(solution)/shard_map/eq | solution.py:153
  123.4 2.9 %compare_convert_fusion.pick_ref = bf16[8,4,128,144]{3,2,1,0:T(8,128)(2,1)S(1)} fusion(f32[8,4,128,144]{3,2,1,0:T(8,128)} %copy.88, f32[144]{0:T(256)S(1)} %eq.55), kind=kLoop, calls=%fused_computation | loop fusion | flops 1179648 | bytes 3539520 | tf_op jit(solution)/shard_map/convert_element_type | solution.py:147
  126.3 4.0 %fusion.6 = bf16[8,144,64]{1,2,0:T(8,128)(2,1)S(1)} fusion(bf16[2048,8,64]{0,2,1:T(8,128)(2,1)S(1)} %bitcast.70, bf16[8,144,2048]{2,1,0:T(8,128)(2,1)} %param.17), kind=kOutput, calls=%fused_computation.18 | convolution fusion | flops 302063616 | bytes 6963200 | tf_op jit(solution)/shard_map/esf,fer->esr/dot_general | solution.py:169
  130.3 0.2 copy.80
  130.5 0.1 copy.81
  130.6 0.2 copy.82
  130.8 10.6 %all_gather.21 = bf16[4,8,144,64]{2,3,1,0:T(8,128)(2,1)S(1)} all-gather(bf16[1,8,144,64]{2,3,1,0:T(8,128)(2,1)S(1)} %copy.82), channel_id=1, replica_groups=mesh['dp'=4,'expert'=8] {'dp'}, dimensions={0}, use_global_device_ids=true | all-gather | bytes 737280 | tf_op jit(solution)/shard_map/all_gather | solution.py:176
  141.4 1.5 copy.83
  142.9 1.8 multiply_convert_fusion.codes_ref
  144.7 17.6 %all-gather.7.cloned.1.call-done = bf16[32,128,896]{2,1,0:T(8,128)(2,1)} async-done(((bf16[4,128,896]{2,1,0:T(8,128)(2,1)}), bf16[32,128,896]{2,1,0:T(8,128)(2,1)}) %all-gather.7.cloned.1.call-update) | async-done | bytes 7340048 | tf_op jit(solution)/shard_map/all_gather | solution.py:167
  162.3 3.1 %copy-done = bf16[32,128,896]{2,1,0:T(8,128)(2,1)S(1)} copy-done((bf16[32,128,896]{2,1,0:T(8,128)(2,1)S(1)}, bf16[32,128,896]{2,1,0:T(8,128)(2,1)}, u32[]{:S(2)}) %copy-start) | copy-done | bytes 7340056
  165.4 1.2 copy-done.2
  166.6 9.1 %project.1 = f32[4,8,144,64]{3,2,1,0:T(8,128)S(1)} custom-call(bf16[8,4,128,896]{3,2,1,0:T(8,128)(2,1)S(1)} %bitcast.64, bf16[896,512]{1,0:T(8,128)(2,1)S(1)} %copy-done.2, bf16[8,4,128,144]{3,2,1,0:T(8,128)(2,1)S(1)} %compare_convert_fusion.pick_ref), custom_call_target="tpu_custom_call" | custom-call | flops 3758096384 | bytes 7340032 | tf_op jit(solution)/shard_map/project/pallas_call | solution.py:189
  175.7 1.6 constant_dynamic-slice_fusion.4
  177.3 2.8 %copy.90 = f32[2,1,8,144,64]{3,4,2,0,1:T(8,128)} copy(f32[2,1,8,144,64]{4,3,2,1,0:T(8,128)} %get-tuple-element.19) | data formatting | bytes 1179648 | tf_op jit(solution)/shard_map/jit(dynamic_index_in_dim)/dynamic_slice | solution.py:97
  180.2 2.9 %copy.89 = f32[2,1,8,144,64]{3,4,2,0,1:T(8,128)} copy(f32[2,1,8,144,64]{4,3,2,1,0:T(8,128)} %get-tuple-element.18) | data formatting | bytes 1179648 | tf_op jit(solution)/shard_map/jit(dynamic_index_in_dim)/dynamic_slice | solution.py:98
  183.1 0.1 collective-permute-done
  183.2 2.7 %bitcast_add_fusion.1 = f32[2,8,144,64]{2,3,1,0:T(8,128)} fusion(f32[2,8,144,64]{2,3,1,0:T(8,128)} %collective-permute-done, f32[2,1,8,144,64]{3,4,2,0,1:T(8,128)} %copy.89), kind=kLoop, calls=%fused_computation.22 | loop fusion | flops 147456 | bytes 1769472 | tf_op jit(solution)/shard_map/add | solution.py:99
  185.8 4.6 %all-to-all-start.1 = ((f32[2,8,144,64]{2,3,1,0:T(8,128)}), f32[2,8,144,64]{2,3,1,0:T(8,128)}, u32[]{:S(2)}, u32[]{:S(2)}) async-start(f32[2,8,144,64]{2,3,1,0:T(8,128)} %bitcast_add_fusion.1), calls=%async_computation.1 | async-start | bytes 2097152 | tf_op jit(solution)/shard_map/all_to_all | solution.py:101
  190.4 0.1 mul.90
  190.5 0.1 copy.93
  190.6 14.1 %all-to-all-done.1 = f32[2,8,144,64]{2,3,1,0:T(8,128)} async-done(((f32[2,8,144,64]{2,3,1,0:T(8,128)}), f32[2,8,144,64]{2,3,1,0:T(8,128)}, u32[]{:S(2)}, u32[]{:S(2)}) %all-to-all-start.1) | async-done | bytes 589856 | tf_op jit(solution)/shard_map/all_to_all | solution.py:101
  204.8 2.2 reduce_sum.50
  206.9 2.1 copy.92
  209.1 1.3 fusion.9
  210.3 0.1 copy.94
  210.4 5.3 %convolution_bitcast_fusion = f32[2048,8,64]{0,2,1:T(8,128)} fusion(bf16[8,144,2048]{2,1,0:T(8,128)(2,1)} %param.17, bf16[8,144,64]{2,0,1:T(8,128)(2,1)S(1)} %bitcast.69), kind=kOutput, calls=%fused_computation.1 | convolution fusion | flops 301989888 | bytes 9060352 | tf_op jit(solution)/shard_map/esf,esr->fer/dot_general | solution.py:222
  215.7 6.6 %reshape_reshape.3 = f32[2,2,512,512]{2,1,0,3:T(2,128)} reshape(f32[2048,8,64]{0,2,1:T(8,128)} %convolution_bitcast_fusion) | data formatting | bytes 8388608 | tf_op jit(solution)/shard_map/reshape;reshape | solution.py:96
  222.3 7.9 %constant_dynamic-slice_fusion.1 = (f32[2,1,512,512]{2,1,0,3:T(1,128)S(1)}, f32[2,1,512,512]{2,1,0,3:T(1,128)S(1)}) fusion(f32[2,2,512,512]{2,1,0,3:T(2,128)} %reshape_reshape.3, s32[]{:T(128)S(6)} %select_n.44, s32[]{:T(128)S(6)} %select_n.45), kind=kLoop, calls=%fused_computation.38 | loop fusion | bytes 8388616 | tf_op jit(solution)/shard_map/jit(dynamic_index_in_dim)/dynamic_slice | solution.py:98
  230.2 0.4 copy.110
  230.6 0.1 collective-permute-start.1
  230.7 4.1 %collective-permute-done.1 = f32[2,512,512]{1,2,0:T(8,128)S(1)} collective-permute-done((f32[2,512,512]{1,2,0:T(8,128)S(1)}, f32[2,512,512]{1,2,0:T(8,128)S(1)}, u32[]{:S(2)}, u32[]{:S(2)}) %collective-permute-start.1) | collective-permute-done | bytes 2097184 | tf_op jit(solution)/shard_map/ppermute | solution.py:99
  234.8 1.4 fusion
  236.2 4.4 %all-to-all-start.2 = ((bf16[2,512,512]{1,2,0:T(8,128)(2,1)}), bf16[2,512,512]{1,2,0:T(8,128)(2,1)}, u32[]{:S(2)}, u32[]{:S(2)}) async-start(bf16[2,512,512]{1,2,0:T(8,128)(2,1)} %fusion), calls=%async_computation.2 | async-start | bytes 2097152 | tf_op jit(solution)/shard_map/all_to_all | solution.py:101
  240.6 3.1 %copy-done.1 = bf16[32,128,896]{2,1,0:T(8,128)(2,1)S(1)} copy-done((bf16[32,128,896]{2,1,0:T(8,128)(2,1)S(1)}, bf16[32,128,896]{2,1,0:T(8,128)(2,1)}, u32[]{:S(2)}) %copy-start.1) | copy-done | bytes 7340056
  243.7 8.9 %outer.1 = f32[896,512]{1,0:T(8,128)} custom-call(bf16[8,4,128,896]{3,2,1,0:T(8,128)(2,1)S(1)} %bitcast.65, bf16[4,8,144,64]{3,2,1,0:T(8,128)(2,1)S(1)} %multiply_convert_fusion.codes_ref, bf16[8,4,128,144]{3,2,1,0:T(8,128)(2,1)S(1)} %compare_convert_fusion.pick_ref), custom_call_target="tpu_custom_call" | custom-call | flops 3758096384 | bytes 7340032 | tf_op jit(solution)/shard_map/outer/pallas_call | solution.py:212
  252.6 2.3 all-to-all-done.2
  254.9 1.5 convert_reduce_fusion
  256.4 1.3 copy.99
  (30 shorter events, 0.1 us)
Async XLA Ops:
  7.2 5.0 %copy-start.4 = (bf16[128,3584]{1,0:T(8,128)(2,1)S(1)}, bf16[128,3584]{1,0:T(8,128)(2,1)}, u32[]{:S(2)}) copy-start(bf16[128,3584]{1,0:T(8,128)(2,1)} %param.14) | copy-start | bytes 2752516
  7.2 5.6 %copy-start.5 = (bf16[128,3584]{1,0:T(8,128)(2,1)S(1)}, bf16[128,3584]{1,0:T(8,128)(2,1)}, u32[]{:S(2)}) copy-start(bf16[128,3584]{1,0:T(8,128)(2,1)} %param.15) | copy-start | bytes 2752516
  7.2 37.8 %all-gather.5.cloned.1.call-start = ((), (), s32[]{:S(2)}) async-start(), calls=%async_computation.3 | async-start | bytes 2621440 | tf_op jit(solution)/shard_map/all_gather | solution.py:165
  9.4 4.0 %copy-start.9 = (s32[128]{0:T(128)S(1)}, s32[128]{0:T(128)}, u32[]{:S(2)}) copy-start(s32[128]{0:T(128)} %param.13) | copy-start | bytes 1540
  9.4 4.0 %copy-start.6 = (f32[3584]{0:T(1024)S(1)}, f32[3584]{0:T(1024)}, u32[]{:S(2)}) copy-start(f32[3584]{0:T(1024)} %param.16) | copy-start | bytes 43012
  9.4 152.9 %all-gather.7.cloned.1.call-start = ((), (), s32[]{:S(2)}) async-start(), calls=%async_computation.4 | async-start | bytes 8257536 | tf_op jit(solution)/shard_map/all_gather | solution.py:167
  15.1 31.3 %copy-start.7 = (s32[128,8]{0,1:T(8,128)S(1)}, s32[128,8]{0,1:T(8,128)}, u32[]{:S(2)}) copy-start(s32[128,8]{0,1:T(8,128)} %param.10) | copy-start | bytes 12292
  15.1 31.3 %copy-start.8 = (f32[128,8]{0,1:T(8,128)S(1)}, f32[128,8]{0,1:T(8,128)}, u32[]{:S(2)}) copy-start(f32[128,8]{0,1:T(8,128)} %param.11) | copy-start | bytes 12292
  123.4 2.9 %copy-start.3 = (bf16[2048,512]{0,1:T(8,128)(2,1)S(1)}, bf16[2048,512]{0,1:T(8,128)(2,1)}, u32[]{:S(2)}) copy-start(bf16[2048,512]{0,1:T(8,128)(2,1)} %all-gather.5.cloned.1.call-done) | copy-start | bytes 6291460
  162.3 3.1 %copy-start = (bf16[32,128,896]{2,1,0:T(8,128)(2,1)S(1)}, bf16[32,128,896]{2,1,0:T(8,128)(2,1)}, u32[]{:S(2)}) copy-start(bf16[32,128,896]{2,1,0:T(8,128)(2,1)} %all-gather.7.cloned.1.call-done) | copy-start | bytes 22020100
  165.4 1.2 copy-start.2
  180.2 3.0 %collective-permute-start = (f32[2,8,144,64]{2,3,1,0:T(8,128)}, f32[2,8,144,64]{2,3,1,0:T(8,128)}, u32[]{:S(2)}, u32[]{:S(2)}) collective-permute-start(f32[2,8,144,64]{2,3,1,0:T(8,128)} %bitcast.74), channel_id=1, source_target_pairs={{0,8},{8,0},{16,24},{24,16},{1,9},{9,1},{17,25},{25,17},{2,10},{10... | collective-permute-start | bytes 1769480 | tf_op jit(solution)/shard_map/ppermute | solution.py:99
  185.8 19.0 %all-to-all-start.1 = ((f32[2,8,144,64]{2,3,1,0:T(8,128)}), f32[2,8,144,64]{2,3,1,0:T(8,128)}, u32[]{:S(2)}, u32[]{:S(2)}) async-start(f32[2,8,144,64]{2,3,1,0:T(8,128)} %bitcast_add_fusion.1), calls=%async_computation.1 | async-start | bytes 2097152 | tf_op jit(solution)/shard_map/all_to_all | solution.py:101
  230.6 4.2 %collective-permute-start.1 = (f32[2,512,512]{1,2,0:T(8,128)S(1)}, f32[2,512,512]{1,2,0:T(8,128)S(1)}, u32[]{:S(2)}, u32[]{:S(2)}) collective-permute-start(f32[2,512,512]{1,2,0:T(8,128)S(1)} %bitcast.71), channel_id=1, source_target_pairs={{0,8},{8,0},{16,24},{24,16},{1,9},{9,1},{17,25},{25,17},{2,10},{10... | collective-permute-start | bytes 6291464 | tf_op jit(solution)/shard_map/ppermute | solution.py:99
  236.2 18.7 %all-to-all-start.2 = ((bf16[2,512,512]{1,2,0:T(8,128)(2,1)}), bf16[2,512,512]{1,2,0:T(8,128)(2,1)}, u32[]{:S(2)}, u32[]{:S(2)}) async-start(bf16[2,512,512]{1,2,0:T(8,128)(2,1)} %fusion), calls=%async_computation.2 | async-start | bytes 2097152 | tf_op jit(solution)/shard_map/all_to_all | solution.py:101
  240.6 3.1 %copy-start.1 = (bf16[32,128,896]{2,1,0:T(8,128)(2,1)S(1)}, bf16[32,128,896]{2,1,0:T(8,128)(2,1)}, u32[]{:S(2)}) copy-start(bf16[32,128,896]{2,1,0:T(8,128)(2,1)} %all-gather.7.cloned.1.call-done) | copy-start | bytes 22020100
Sparse Core Ops, SparseCore 0:
  10.2 34.7 all-gather.4
  47.7 114.5 all-gather.6

commit v3 on v2

--- a/solution.py
+++ b/solution.py
@@ -62,7 +62,19 @@
         total = chosen[:, :rank]
         for e in range(1, experts_here):
             total += chosen[:, e * rank : (e + 1) * rank]
-        back_ref[p, 0] = total
+        back_ref[p, 0] = jnp.concatenate([total[: rows // 2], total[rows // 2 :]], axis=1)
+
+
+def inner_kernel(hidden_ref, back_ref, grad_ref):
+    grad_ref[...] = jnp.concatenate(
+        [
+            lax.dot_general(
+                hidden_ref[k], back_ref[k], (((0,), (0,)), ((), ())), preferred_element_type=F32
+            )
+            for k in range(hidden_ref.shape[0])
+        ],
+        axis=1,
+    )
 
 
 def outer_kernel(experts_here, cot_ref, codes_ref, pick_ref, grad_ref):
@@ -102,6 +114,18 @@
         kept.astype(wire), "dp", split_axis=0, concat_axis=0, axis_index_groups=groups, tiled=True
     )
     return jnp.sum(landed.astype(F32), axis=0)
+
+
+def gather_rows(shard):
+    data = lax.axis_size("dp")
+    me = lax.axis_index("dp")
+    pieces = [shard] + [
+        lax.ppermute(shard, "dp", [((i + k) % data, i) for i in range(data)])
+        for k in range(1, data)
+    ]
+    start = lax.rem(data - me, data) * shard.shape[0]
+    twice = jnp.concatenate(pieces + pieces[:-1], axis=0)
+    return lax.dynamic_slice_in_dim(twice, start, data * shard.shape[0], axis=0)
 
 
 def local(
@@ -162,8 +186,8 @@
     ).astype(BF16)
     cotangent = cotangent.reshape(tokens, data, depth).transpose(1, 0, 2)
     cotangent = lax.all_to_all(cotangent, "dp", split_axis=0, concat_axis=0, tiled=True)
-    in_factor = lax.all_gather(adapter_in, "dp", axis=0, tiled=True)
-    cotangent, in_factor = lax.optimization_barrier((cotangent, in_factor))
+    cotangent, adapter_in = lax.optimization_barrier((cotangent, adapter_in))
+    in_factor = gather_rows(adapter_in)
     cotangent = lax.all_gather(cotangent, "expert", axis=0, tiled=False)
 
     codes = jnp.einsum(
@@ -194,13 +218,15 @@
             pl.BlockSpec((depth, width), lambda i: (0, 0)),
             pick_spec,
         ],
-        out_specs=slot_spec,
-        out_shape=jax.ShapeDtypeStruct((data, along, rows, rank), F32),
+        out_specs=pl.BlockSpec((data, 1, rows // 2, 2 * rank), lambda i: (0, i, 0, 0)),
+        out_shape=jax.ShapeDtypeStruct((data, along, rows // 2, 2 * rank), F32),
         compiler_params=params,
         cost_estimate=cost,
         name="project",
     )(cotangent, adapter_out, pick)
-    back = sum_over_data(back, F32)
+    back = lax.all_to_all(back, "dp", split_axis=0, concat_axis=0, tiled=True)
+    back = jnp.sum(back, axis=0).reshape(along, rows // 2, 2, rank)
+    back = back.transpose(0, 2, 1, 3).reshape(along, rows, rank)
     own_gate = lax.dynamic_index_in_dim(slot_gate, lax.axis_index("dp"), 1, keepdims=False)
     back = (
         (back * own_gate)
@@ -219,7 +245,18 @@
         cost_estimate=cost,
         name="outer",
     )(cotangent, codes, pick)
-    product = jnp.einsum("esf,esr->fer", saved_hidden, back, preferred_element_type=F32)
+    product = pl.pallas_call(
+        inner_kernel,
+        grid=(experts_here // 2,),
+        in_specs=[
+            pl.BlockSpec((2, slot_count, hidden_width), lambda i: (i, 0, 0)),
+            pl.BlockSpec((2, slot_count, rank), lambda i: (i, 0, 0)),
+        ],
+        out_specs=pl.BlockSpec((hidden_width, 2 * rank), lambda i: (0, i)),
+        out_shape=jax.ShapeDtypeStruct((hidden_width, width), F32),
+        compiler_params=params,
+        name="inner",
+    )(saved_hidden, back)
     grad_in = sum_over_data(product.reshape(data, hidden_width // data, width), BF16)
     return (grad_in, grad_out)
 

time: 266 us -> 252 us (0.947)
  blocking collectives: 109 us -> 97.3 us
  Pallas kernels: 18 us -> 22.7 us
  matrix products: 9.54 us -> 4.91 us
  local copies, waits for them, and re-layouts: 44.2 us -> 41.3 us
    ppermute x0 -> x3, waiting for transfers between devices: none -> 19.7 us  [gather_rows(): lax.ppermute(shard, 'dp', [((i + k) % data, i) for i in range(data)])]
    all_gather x1, waiting for transfers between devices: 17.6 us -> 0.02 us  [local(): cotangent = lax.all_gather(cotangent, 'expert', axis=0, tiled=False)]
    all_to_all x0 -> x1, waiting for transfers between devices: none -> 15.5 us  [local(): back = lax.all_to_all(back, 'dp', split_axis=0, concat_axis=0, tiled=True)]
    all_to_all x2 -> x1, waiting for transfers between devices: 16.4 us -> 2.28 us  [sum_over_data(): lax.all_to_all(kept.astype(wire), 'dp', split_axis=0, concat_axis=0, axis...]
    dynamic_slice x5 -> x2, local copies, waits for them, and re-layouts: 15.7 us -> 5.53 us  [gather_rows(): return lax.dynamic_slice_in_dim(twice, start, data * shard.shape[0], axis=0)]
    all_to_all x1, blocking collectives: 26.9 us -> 17.1 us  [local(): lax.all_to_all(cotangent, 'dp', split_axis=0, concat_axis=0, tiled=True)]
    another operation x1 -> x0, local copies, waits for them, and re-layouts: 6.59 us -> none  [sum_over_data(): pairs = terms.reshape((data // 2, 2) + terms.shape[1:])]
    dot_general x1 -> x0, matrix products: 5.26 us -> none  [local(): jnp.einsum('esf,esr->fer', saved_hidden, back, preferred_element_type=F32)]
  transfers between devices with their start and end apart: 6 -> 7, of which waited for: 6 -> 5; matrix products, arithmetic and copies ran while one was open for 9% -> 13% of each run, Pallas kernels for 3% -> 4%
where the time goes in v3:
time: 252 us; the launch traced here: 251 us
  blocking collectives  97.3 us (39%)
  waiting for transfers between devices  42 us (17%)
  local copies, waits for them, and re-layouts  41.3 us (16%)
  Pallas kernels  22.7 us (9%)
  other arithmetic  17.3 us (7%)
  between operations  15.2 us (6%)
  starting transfers between devices  10.4 us (4%)
  matrix products  4.91 us (2%)
    all_gather x1, blocking collectives, local(): info = lax.all_gather(info, ('dp', 'expert'), axis=0, tiled=False)  71.2 us
    ppermute x3, waiting for transfers between devices, gather_rows(): lax.ppermute(shard, 'dp', [((i + k) % data, i) for i in range(data)])  19.7 us
    unnamed x37, local copies, waits for them, and re-layouts  17.4 us
    all_to_all x1, blocking collectives, local(): lax.all_to_all(cotangent, 'dp', split_axis=0, concat_axis=0, tiled=True)  17.1 us
    all_to_all x1, waiting for transfers between devices, local(): back = lax.all_to_all(back, 'dp', split_axis=0, concat_axis=0, tiled=True)  15.5 us
    pallas_call x1, Pallas kernels, local(): pl.pallas_call(functools.partial(project_kernel, experts_here), grid=(alo...  9.67 us
    all_gather x1, blocking collectives, local(): lax.all_gather(codes.reshape(along, rows, rank), 'dp', axis=0, tiled=False)  9.07 us
    pallas_call x1, Pallas kernels, local(): pl.pallas_call(functools.partial(outer_kernel, experts_here), grid=(along...  8.89 us
  transfers between devices with their start and end apart: 7, of which 5 were waited for; matrix products, arithmetic and copies ran while one was open for 13% of the time, Pallas kernels for 4%

profile of v3, /device:TPU:0, one launch (start us, length us, event | category | flops | bytes accessed | tf_op | source)
XLA Modules:
  0.0 251.1 jit_solution(9799838349356871285)
XLA Ops:
  7.2 0.0 all-gather.4.cloned.1.call-start
  7.3 1.6 copy.63
  8.9 0.6 copy.64
  9.5 0.6 multiply_reduce_fusion
  10.9 1.6 fusion.4
  12.5 17.1 %all_to_all.15 = bf16[4,128,896]{1,2,0:T(8,128)(2,1)S(1)} all-to-all(bf16[4,128,896]{1,2,0:T(8,128)(2,1)S(1)} %bitcast.61), channel_id=1, replica_groups=mesh['dp'=4,'expert'=8] {'dp'}, dimensions={0} | all-to-all | bytes 1835008 | tf_op jit(solution)/shard_map/all_to_all | solution.py:188
  29.6 1.3 copy.65
  30.9 71.2 %all-gather.1 = f32[4096,16]{0,1:T(8,128)S(1)} all-gather(f32[128,16]{0,1:T(8,128)S(1)} %pad_maximum_fusion), channel_id=3, replica_groups=mesh['dp'=4,'expert'=8] {'dp','expert'}, dimensions={0}, use_global_device_ids=true | all-gather | bytes 270336 | tf_op jit(solution)/shard_map/all_gather | solution.py:155
  102.1 0.1 copy.81
  102.1 0.2 copy.83
  102.4 0.3 compare_reduce_fusion
  102.6 0.2 fusion.7
  102.9 0.1 copy.72
  103.0 1.7 eq.49
  104.7 4.8 %copy.75 = f32[8,4,128,144]{3,2,1,0:T(8,128)} copy(f32[8,4,128,144]{2,0,3,1:T(8,128)} %bitcast.59) | data formatting | bytes 4718592 | tf_op jit(solution)/shard_map/eq | solution.py:177
  109.5 0.1 eq.54
  109.6 0.2 fusion.8
  109.8 2.8 %compare_convert_fusion.pick_ref = bf16[8,4,128,144]{3,2,1,0:T(8,128)(2,1)S(1)} fusion(f32[8,4,128,144]{3,2,1,0:T(8,128)} %copy.75, f32[144]{0:T(256)S(1)} %eq.54), kind=kLoop, calls=%fused_computation | loop fusion | flops 1179648 | bytes 3539520 | tf_op jit(solution)/shard_map/convert_element_type | solution.py:171
  112.6 0.1 collective-permute-start
  112.6 1.2 collective-permute-start.1
  113.9 0.1 copy.73
  114.0 0.2 collective-permute-start.2
  114.2 1.7 select_reduce_fusion
  115.9 0.9 copy.74
  116.8 1.0 reshape.60
  117.8 6.4 %collective-permute-done = bf16[512,512]{1,0:T(8,128)(2,1)S(1)} collective-permute-done((bf16[512,512]{1,0:T(8,128)(2,1)S(1)}, bf16[512,512]{1,0:T(8,128)(2,1)S(1)}, u32[]{:S(2)}, u32[]{:S(2)}) %collective-permute-start) | collective-permute-done | bytes 524320 | tf_op jit(solution)/shard_map/ppermute | solution.py:123
  124.3 13.2 %collective-permute-done.1 = bf16[512,512]{1,0:T(8,128)(2,1)} collective-permute-done((bf16[512,512]{1,0:T(8,128)(2,1)S(1)}, bf16[512,512]{1,0:T(8,128)(2,1)}, u32[]{:S(2)}, u32[]{:S(2)}) %collective-permute-start.1) | collective-permute-done | bytes 524320 | tf_op jit(solution)/shard_map/ppermute | solution.py:123
  137.6 1.1 constant_dynamic-update-slice_fusion.4
  138.7 1.1 constant_dynamic-update-slice_fusion.3
  139.8 1.1 constant_dynamic-update-slice_fusion
  140.9 1.5 constant_dynamic-slice_fusion.1
  142.4 4.0 %copy.66 = bf16[2048,512]{0,1:T(8,128)(2,1)} copy(bf16[2048,512]{1,0:T(8,128)(2,1)} %constant_dynamic-slice_fusion.1) | data formatting | bytes 4194304 | tf_op jit(solution)/shard_map/dynamic_slice | solution.py:128
  146.4 4.7 %fusion.6 = bf16[8,144,64]{1,2,0:T(8,128)(2,1)S(1)} fusion(bf16[2048,8,64]{0,2,1:T(8,128)(2,1)} %bitcast.60, bf16[8,144,2048]{2,1,0:T(8,128)(2,1)} %hidden_ref.1), kind=kOutput, calls=%fused_computation.17 | convolution fusion | flops 302063616 | bytes 6963200 | tf_op jit(solution)/shard_map/esf,fer->esr/dot_general | solution.py:193
  151.1 0.2 copy.67
  151.3 0.1 copy.68
  151.4 0.2 copy.69
  151.7 9.1 %all_gather.17 = bf16[4,8,144,64]{2,3,1,0:T(8,128)(2,1)S(1)} all-gather(bf16[1,8,144,64]{2,3,1,0:T(8,128)(2,1)S(1)} %copy.69), channel_id=1, replica_groups=mesh['dp'=4,'expert'=8] {'dp'}, dimensions={0}, use_global_device_ids=true | all-gather | bytes 737280 | tf_op jit(solution)/shard_map/all_gather | solution.py:200
  160.7 1.5 copy.70
  162.2 1.8 multiply_convert_fusion.codes_ref
  164.1 0.0 all-gather.4.cloned.1.call-done
  164.1 3.1 %copy-done.3 = bf16[32,128,896]{2,1,0:T(8,128)(2,1)S(1)} copy-done((bf16[32,128,896]{2,1,0:T(8,128)(2,1)S(1)}, bf16[32,128,896]{2,1,0:T(8,128)(2,1)}, u32[]{:S(2)}) %copy-start.3) | copy-done | bytes 7340056
  167.2 1.2 copy-done.5
  168.4 9.7 %project.1 = f32[4,8,72,128]{3,2,1,0:T(8,128)S(1)} custom-call(bf16[8,4,128,896]{3,2,1,0:T(8,128)(2,1)S(1)} %bitcast.57, bf16[896,512]{1,0:T(8,128)(2,1)S(1)} %copy-done.5, bf16[8,4,128,144]{3,2,1,0:T(8,128)(2,1)S(1)} %compare_convert_fusion.pick_ref), custom_call_target="tpu_custom_call" | custom-call | flops 3758096384 | bytes 7340032 | tf_op jit(solution)/shard_map/project/pallas_call | solution.py:213
  178.1 1.0 copy-done.2
  179.1 4.4 %all-to-all-start.1 = ((f32[4,8,72,128]{3,2,1,0:T(8,128)}), f32[4,8,72,128]{3,2,1,0:T(8,128)}, u32[]{:S(2)}, u32[]{:S(2)}) async-start(f32[4,8,72,128]{3,2,1,0:T(8,128)} %copy-done.2), calls=%async_computation.1 | async-start | bytes 2359296 | tf_op jit(solution)/shard_map/all_to_all | solution.py:227
  183.5 0.1 mul.94
  183.6 0.1 copy.77
  183.7 15.5 %all-to-all-done.1 = f32[4,8,72,128]{3,2,1,0:T(8,128)} async-done(((f32[4,8,72,128]{3,2,1,0:T(8,128)}), f32[4,8,72,128]{3,2,1,0:T(8,128)}, u32[]{:S(2)}, u32[]{:S(2)}) %all-to-all-start.1) | async-done | bytes 1179680 | tf_op jit(solution)/shard_map/all_to_all | solution.py:227
  199.3 2.1 reduce_sum.48
  201.3 2.1 reshape.61
  203.5 1.3 copy.76
  204.7 0.2 fusion.9
  205.0 0.1 copy.78
  205.1 2.3 copy-done
  207.4 4.1 %inner.1 = f32[2048,512]{1,0:T(8,128)S(1)} custom-call(bf16[8,144,2048]{2,1,0:T(8,128)(2,1)S(1)} %copy-done, bf16[8,144,64]{2,1,0:T(8,128)(2,1)S(1)} %copy.79.back_ref), custom_call_target="tpu_custom_call" | custom-call | tf_op jit(solution)/shard_map/inner/pallas_call | solution.py:248
  211.6 2.1 copy-done.1
  213.6 1.5 dynamic-slice_bitcast_fusion
  215.1 4.5 %collective-permute-done.3 = f32[2,512,512]{2,1,0:T(8,128)} collective-permute-done((f32[2,512,512]{2,1,0:T(8,128)}, f32[2,512,512]{2,1,0:T(8,128)}, u32[]{:S(2)}, u32[]{:S(2)}) %collective-permute-start.3) | collective-permute-done | bytes 2097184 | tf_op jit(solution)/shard_map/ppermute | solution.py:111
  219.6 3.5 %fusion = bf16[2,512,512]{2,1,0:T(8,128)(2,1)} fusion(f32[2,512,512]{2,1,0:T(8,128)} %collective-permute-done.3, f32[2,2,512,512]{3,2,1,0:T(8,128)} %bitcast.56, s32[]{:T(128)S(6)} %select_n.44), kind=kLoop, calls=%fused_computation.6 | loop fusion | flops 1048576 | bytes 5242884 | tf_op jit(solution)/shard_map/convert_element_type | solution.py:114
  223.2 4.4 %all-to-all-start.2 = ((bf16[2,512,512]{2,1,0:T(8,128)(2,1)}), bf16[2,512,512]{2,1,0:T(8,128)(2,1)}, u32[]{:S(2)}, u32[]{:S(2)}) async-start(bf16[2,512,512]{2,1,0:T(8,128)(2,1)} %fusion), calls=%async_computation.2 | async-start | bytes 2097152 | tf_op jit(solution)/shard_map/all_to_all | solution.py:113
  227.6 3.1 %copy-done.4 = bf16[32,128,896]{2,1,0:T(8,128)(2,1)S(1)} copy-done((bf16[32,128,896]{2,1,0:T(8,128)(2,1)S(1)}, bf16[32,128,896]{2,1,0:T(8,128)(2,1)}, u32[]{:S(2)}) %copy-start.4) | copy-done | bytes 7340056
  230.7 8.9 %outer.1 = f32[896,512]{1,0:T(8,128)} custom-call(bf16[8,4,128,896]{3,2,1,0:T(8,128)(2,1)S(1)} %bitcast.58, bf16[4,8,144,64]{3,2,1,0:T(8,128)(2,1)S(1)} %multiply_convert_fusion.codes_ref, bf16[8,4,128,144]{3,2,1,0:T(8,128)(2,1)S(1)} %compare_convert_fusion.pick_ref), custom_call_target="tpu_custom_call" | custom-call | flops 3758096384 | bytes 7340032 | tf_op jit(solution)/shard_map/outer/pallas_call | solution.py:238
  239.5 2.3 all-to-all-done.2
  241.8 2.5 convert_reduce_fusion
  (42 shorter events, 0.3 us)
Async XLA Ops:
  7.2 1.7 copy-start.8
  7.2 2.3 copy-start.9
  7.2 3.6 %copy-start.12 = (s32[128]{0:T(128)S(1)}, s32[128]{0:T(128)}, u32[]{:S(2)}) copy-start(s32[128]{0:T(128)} %param.12) | copy-start | bytes 1540
  7.2 3.7 %copy-start.13 = (s32[128]{0:T(128)S(1)}, s32[128]{0:T(128)}, u32[]{:S(2)}) copy-start(s32[128]{0:T(128)} %param.13) | copy-start | bytes 1540
  7.2 156.9 %all-gather.4.cloned.1.call-start = ((), (), s32[]{:S(2)}) async-start(), calls=%async_computation.3 | async-start | bytes 8257536 | tf_op jit(solution)/shard_map/all_gather | solution.py:191
  12.5 18.4 %copy-start.10 = (s32[128,8]{0,1:T(8,128)S(1)}, s32[128,8]{0,1:T(8,128)}, u32[]{:S(2)}) copy-start(s32[128,8]{0,1:T(8,128)} %param.10) | copy-start | bytes 12292
  12.5 18.4 %copy-start.11 = (f32[128,8]{0,1:T(8,128)S(1)}, f32[128,8]{0,1:T(8,128)}, u32[]{:S(2)}) copy-start(f32[128,8]{0,1:T(8,128)} %param.11) | copy-start | bytes 12292
  102.9 6.5 %copy-start.7 = (f32[8,4,128,8]{2,0,3,1:T(8,128)}, f32[8,4,128,8]{2,0,3,1:T(8,128)S(1)}, u32[]{:S(2)}) copy-start(f32[8,4,128,8]{2,0,3,1:T(8,128)S(1)} %copy.72) | copy-start | bytes 393220
  109.8 2.8 %copy-start.6 = (bf16[512,512]{1,0:T(8,128)(2,1)S(1)}, bf16[512,512]{1,0:T(8,128)(2,1)}, u32[]{:S(2)}) copy-start(bf16[512,512]{1,0:T(8,128)(2,1)} %param.18) | copy-start | bytes 1572868
  112.6 11.7 %collective-permute-start = (bf16[512,512]{1,0:T(8,128)(2,1)S(1)}, bf16[512,512]{1,0:T(8,128)(2,1)S(1)}, u32[]{:S(2)}, u32[]{:S(2)}) collective-permute-start(bf16[512,512]{1,0:T(8,128)(2,1)S(1)} %copy-done.6), channel_id=1, source_target_pairs={{8,0},{16,8},{24,16},{0,24},{9,1},{17,9},{25,17},{1,25},{10,2},{18... | collective-permute-start | bytes 1572872 | tf_op jit(solution)/shard_map/ppermute | solution.py:123
  112.6 24.9 %collective-permute-start.1 = (bf16[512,512]{1,0:T(8,128)(2,1)S(1)}, bf16[512,512]{1,0:T(8,128)(2,1)}, u32[]{:S(2)}, u32[]{:S(2)}) collective-permute-start(bf16[512,512]{1,0:T(8,128)(2,1)S(1)} %copy-done.6), channel_id=1, source_target_pairs={{16,0},{24,8},{0,16},{8,24},{17,1},{25,9},{1,17},{9,25},{18,2},{26... | collective-permute-start | bytes 1572872 | tf_op jit(solution)/shard_map/ppermute | solution.py:123
  114.0 24.7 %collective-permute-start.2 = (bf16[512,512]{1,0:T(8,128)(2,1)S(1)}, bf16[512,512]{1,0:T(8,128)(2,1)}, u32[]{:S(2)}, u32[]{:S(2)}) collective-permute-start(bf16[512,512]{1,0:T(8,128)(2,1)S(1)} %copy-done.6), channel_id=1, source_target_pairs={{24,0},{0,8},{8,16},{16,24},{25,1},{1,9},{9,17},{17,25},{26,2},{2,... | collective-permute-start | bytes 1572872 | tf_op jit(solution)/shard_map/ppermute | solution.py:123
  164.1 3.1 %copy-start.3 = (bf16[32,128,896]{2,1,0:T(8,128)(2,1)S(1)}, bf16[32,128,896]{2,1,0:T(8,128)(2,1)}, u32[]{:S(2)}) copy-start(bf16[32,128,896]{2,1,0:T(8,128)(2,1)} %all-gather.4.cloned.1.call-done) | copy-start | bytes 22020100
  167.2 1.2 copy-start.5
  178.0 1.0 copy-start.2
  179.1 20.2 %all-to-all-start.1 = ((f32[4,8,72,128]{3,2,1,0:T(8,128)}), f32[4,8,72,128]{3,2,1,0:T(8,128)}, u32[]{:S(2)}, u32[]{:S(2)}) async-start(f32[4,8,72,128]{3,2,1,0:T(8,128)} %copy-done.2), calls=%async_computation.1 | async-start | bytes 2359296 | tf_op jit(solution)/shard_map/all_to_all | solution.py:227
  205.1 2.3 copy-start
  211.6 2.1 copy-start.1
  215.1 4.5 %collective-permute-start.3 = (f32[2,512,512]{2,1,0:T(8,128)}, f32[2,512,512]{2,1,0:T(8,128)}, u32[]{:S(2)}, u32[]{:S(2)}) collective-permute-start(f32[2,512,512]{2,1,0:T(8,128)} %dynamic-slice_bitcast_fusion), channel_id=1, source_target_pairs={{0,8},{8,0},{16,24},{24,16},{1,9},{9,1},{17,25},{25,17},{2,10},{10... | collective-permute-start | bytes 6291464 | tf_op jit(solution)/shard_map/ppermute | solution.py:111
  223.2 18.7 %all-to-all-start.2 = ((bf16[2,512,512]{2,1,0:T(8,128)(2,1)}), bf16[2,512,512]{2,1,0:T(8,128)(2,1)}, u32[]{:S(2)}, u32[]{:S(2)}) async-start(bf16[2,512,512]{2,1,0:T(8,128)(2,1)} %fusion), calls=%async_computation.2 | async-start | bytes 2097152 | tf_op jit(solution)/shard_map/all_to_all | solution.py:113
  227.6 3.1 %copy-start.4 = (bf16[32,128,896]{2,1,0:T(8,128)(2,1)S(1)}, bf16[32,128,896]{2,1,0:T(8,128)(2,1)}, u32[]{:S(2)}) copy-start(bf16[32,128,896]{2,1,0:T(8,128)(2,1)} %all-gather.4.cloned.1.call-done) | copy-start | bytes 22020100
Sparse Core Ops, SparseCore 0:
  31.0 114.5 all-gather.3

commit v4 on v3

--- a/solution.py
+++ b/solution.py
@@ -186,7 +186,6 @@
     ).astype(BF16)
     cotangent = cotangent.reshape(tokens, data, depth).transpose(1, 0, 2)
     cotangent = lax.all_to_all(cotangent, "dp", split_axis=0, concat_axis=0, tiled=True)
-    cotangent, adapter_in = lax.optimization_barrier((cotangent, adapter_in))
     in_factor = gather_rows(adapter_in)
     cotangent = lax.all_gather(cotangent, "expert", axis=0, tiled=False)
 

time: 252 us -> 234 us (0.929)
  waiting for transfers between devices: 42 us -> 25.7 us
  local copies, waits for them, and re-layouts: 41.3 us -> 38.3 us
  blocking collectives: 97.3 us -> 99.9 us
    ppermute x3, waiting for transfers between devices: 19.7 us -> 0.01 us  [gather_rows(): lax.ppermute(shard, 'dp', [((i + k) % data, i) for i in range(data)])]
    all_gather x1, waiting for transfers between devices: 0.02 us -> 3.35 us  [local(): cotangent = lax.all_gather(cotangent, 'expert', axis=0, tiled=False)]
    eq x4, local copies, waits for them, and re-layouts: 6.59 us -> 3.41 us  [local(): place[..., None] == jnp.arange(capacity, dtype=jnp.int32).astype(F32)]
    unnamed x37 -> x39, local copies, waits for them, and re-layouts: 17.4 us -> 18.6 us
  transfers between devices with their start and end apart: 7 -> 7, of which waited for: 5 -> 4; matrix products, arithmetic and copies ran while one was open for 13% -> 12% of each run, Pallas kernels for 4% -> 4%
where the time goes in v4:
time: 234 us; the launch traced here: 233 us
  blocking collectives  99.9 us (43%)
  local copies, waits for them, and re-layouts  38.3 us (16%)
  waiting for transfers between devices  25.7 us (11%)
  Pallas kernels  22.7 us (10%)
  other arithmetic  16.6 us (7%)
  between operations  15.2 us (6%)
  starting transfers between devices  10 us (4%)
  matrix products  4.91 us (2%)
    all_gather x1, blocking collectives, local(): info = lax.all_gather(info, ('dp', 'expert'), axis=0, tiled=False)  73.5 us
    unnamed x39, local copies, waits for them, and re-layouts  18.6 us
    all_to_all x1, blocking collectives, local(): lax.all_to_all(cotangent, 'dp', split_axis=0, concat_axis=0, tiled=True)  17.2 us
    all_to_all x1, waiting for transfers between devices, local(): back = lax.all_to_all(back, 'dp', split_axis=0, concat_axis=0, tiled=True)  15.5 us
    pallas_call x1, Pallas kernels, local(): pl.pallas_call(functools.partial(project_kernel, experts_here), grid=(alo...  9.69 us
    all_gather x1, blocking collectives, local(): lax.all_gather(codes.reshape(along, rows, rank), 'dp', axis=0, tiled=False)  9.21 us
    pallas_call x1, Pallas kernels, local(): pl.pallas_call(functools.partial(outer_kernel, experts_here), grid=(along...  8.89 us
    dynamic_slice x2, local copies, waits for them, and re-layouts, gather_rows(): return lax.dynamic_slice_in_dim(twice, start, data * shard.shape[0], axis=0)  5.46 us
  transfers between devices with their start and end apart: 7, of which 4 were waited for; matrix products, arithmetic and copies ran while one was open for 12% of the time, Pallas kernels for 4%

profile of v4, /device:TPU:0, one launch (start us, length us, event | category | flops | bytes accessed | tf_op | source)
XLA Modules:
  0.0 233.3 jit_solution(1553194028169372056)
XLA Ops:
  7.2 0.0 all-gather.4.cloned.1.call-start
  7.3 1.6 copy.63
  8.9 0.6 copy.64
  9.5 0.6 multiply_reduce_fusion
  10.9 1.6 fusion.4
  12.5 17.2 %all_to_all.15 = bf16[4,128,896]{1,2,0:T(8,128)(2,1)S(1)} all-to-all(bf16[4,128,896]{1,2,0:T(8,128)(2,1)S(1)} %bitcast.61), channel_id=1, replica_groups=mesh['dp'=4,'expert'=8] {'dp'}, dimensions={0} | all-to-all | bytes 1835008 | tf_op jit(solution)/shard_map/all_to_all | solution.py:188
  29.7 1.3 copy.65
  31.0 0.0 all-gather.4.cloned.1.call-update
  31.0 0.1 collective-permute-start
  31.1 1.1 collective-permute-start.1
  32.2 73.5 %all-gather.1 = f32[4096,16]{0,1:T(8,128)S(1)} all-gather(f32[128,16]{0,1:T(8,128)S(1)} %pad_maximum_fusion), channel_id=3, replica_groups=mesh['dp'=4,'expert'=8] {'dp','expert'}, dimensions={0}, use_global_device_ids=true | all-gather | bytes 270336 | tf_op jit(solution)/shard_map/all_gather | solution.py:155
  105.7 0.1 copy.81
  105.8 0.2 copy.83
  106.0 0.2 fusion.8
  106.2 0.1 copy.73
  106.3 0.3 compare_reduce_fusion
  106.5 0.2 fusion.7
  106.8 0.1 copy.72
  106.9 0.8 select_reduce_fusion
  107.7 0.8 constant_dynamic-update-slice_fusion.6
  108.5 0.3 copy.74
  108.8 0.7 reshape.60
  109.5 0.2 eq.49
  109.7 3.2 %copy.75 = f32[8,4,128,144]{3,2,1,0:T(8,128)} copy(f32[8,4,128,144]{2,0,3,1:T(8,128)S(1)} %bitcast.59) | data formatting | bytes 4718592 | tf_op jit(solution)/shard_map/eq | solution.py:177
  112.8 0.1 eq.54
  112.9 3.0 %compare_convert_fusion.pick_ref = bf16[8,4,128,144]{3,2,1,0:T(8,128)(2,1)S(1)} fusion(f32[8,4,128,144]{3,2,1,0:T(8,128)} %copy.75, f32[144]{0:T(256)S(1)} %eq.54), kind=kLoop, calls=%fused_computation | loop fusion | flops 1179648 | bytes 3539520 | tf_op jit(solution)/shard_map/convert_element_type | solution.py:171
  115.9 0.4 copy-done.7
  116.3 1.1 constant_dynamic-update-slice_fusion.4
  117.4 1.1 constant_dynamic-update-slice_fusion.3
  118.6 1.1 constant_dynamic-update-slice_fusion
  119.7 1.5 constant_dynamic-slice_fusion.1
  121.2 3.9 %copy.66 = bf16[2048,512]{0,1:T(8,128)(2,1)} copy(bf16[2048,512]{1,0:T(8,128)(2,1)} %constant_dynamic-slice_fusion.1) | data formatting | bytes 4194304 | tf_op jit(solution)/shard_map/dynamic_slice | solution.py:128
  125.1 4.7 %fusion.6 = bf16[8,144,64]{1,2,0:T(8,128)(2,1)S(1)} fusion(bf16[2048,8,64]{0,2,1:T(8,128)(2,1)} %bitcast.60, bf16[8,144,2048]{2,1,0:T(8,128)(2,1)} %hidden_ref.1), kind=kOutput, calls=%fused_computation.17 | convolution fusion | flops 302063616 | bytes 6963200 | tf_op jit(solution)/shard_map/esf,fer->esr/dot_general | solution.py:192
  129.8 0.2 copy.67
  130.1 0.1 copy.68
  130.1 0.2 copy.69
  130.4 9.2 %all_gather.17 = bf16[4,8,144,64]{2,3,1,0:T(8,128)(2,1)S(1)} all-gather(bf16[1,8,144,64]{2,3,1,0:T(8,128)(2,1)S(1)} %copy.69), channel_id=1, replica_groups=mesh['dp'=4,'expert'=8] {'dp'}, dimensions={0}, use_global_device_ids=true | all-gather | bytes 737280 | tf_op jit(solution)/shard_map/all_gather | solution.py:199
  139.6 1.5 copy.70
  141.1 1.8 multiply_convert_fusion.codes_ref
  142.9 3.3 %all-gather.4.cloned.1.call-done = bf16[32,128,896]{2,1,0:T(8,128)(2,1)} async-done(((bf16[4,128,896]{2,1,0:T(8,128)(2,1)}), bf16[32,128,896]{2,1,0:T(8,128)(2,1)}) %all-gather.4.cloned.1.call-update) | async-done | bytes 7340048 | tf_op jit(solution)/shard_map/all_gather | solution.py:190
  146.3 3.1 %copy-done.3 = bf16[32,128,896]{2,1,0:T(8,128)(2,1)S(1)} copy-done((bf16[32,128,896]{2,1,0:T(8,128)(2,1)S(1)}, bf16[32,128,896]{2,1,0:T(8,128)(2,1)}, u32[]{:S(2)}) %copy-start.3) | copy-done | bytes 7340056
  149.4 1.2 copy-done.5
  150.5 9.7 %project.1 = f32[4,8,72,128]{3,2,1,0:T(8,128)S(1)} custom-call(bf16[8,4,128,896]{3,2,1,0:T(8,128)(2,1)S(1)} %bitcast.57, bf16[896,512]{1,0:T(8,128)(2,1)S(1)} %copy-done.5, bf16[8,4,128,144]{3,2,1,0:T(8,128)(2,1)S(1)} %compare_convert_fusion.pick_ref), custom_call_target="tpu_custom_call" | custom-call | flops 3758096384 | bytes 7340032 | tf_op jit(solution)/shard_map/project/pallas_call | solution.py:212
  160.2 1.0 copy-done.2
  161.2 4.4 %all-to-all-start.1 = ((f32[4,8,72,128]{3,2,1,0:T(8,128)}), f32[4,8,72,128]{3,2,1,0:T(8,128)}, u32[]{:S(2)}, u32[]{:S(2)}) async-start(f32[4,8,72,128]{3,2,1,0:T(8,128)} %copy-done.2), calls=%async_computation.1 | async-start | bytes 2359296 | tf_op jit(solution)/shard_map/all_to_all | solution.py:226
  165.7 0.1 mul.94
  165.8 0.1 copy.77
  165.9 15.5 %all-to-all-done.1 = f32[4,8,72,128]{3,2,1,0:T(8,128)} async-done(((f32[4,8,72,128]{3,2,1,0:T(8,128)}), f32[4,8,72,128]{3,2,1,0:T(8,128)}, u32[]{:S(2)}, u32[]{:S(2)}) %all-to-all-start.1) | async-done | bytes 1179680 | tf_op jit(solution)/shard_map/all_to_all | solution.py:226
  181.4 2.1 reduce_sum.48
  183.5 2.1 reshape.61
  185.7 1.3 copy.76
  186.9 0.2 fusion.9
  187.1 0.1 copy.78
  187.3 2.3 copy-done
  189.6 4.1 %inner.1 = f32[2048,512]{1,0:T(8,128)S(1)} custom-call(bf16[8,144,2048]{2,1,0:T(8,128)(2,1)S(1)} %copy-done, bf16[8,144,64]{2,1,0:T(8,128)(2,1)S(1)} %copy.79.back_ref), custom_call_target="tpu_custom_call" | custom-call | tf_op jit(solution)/shard_map/inner/pallas_call | solution.py:247
  193.8 2.1 copy-done.1
  195.8 1.5 dynamic-slice_bitcast_fusion
  197.3 4.5 %collective-permute-done.3 = f32[2,512,512]{2,1,0:T(8,128)} collective-permute-done((f32[2,512,512]{2,1,0:T(8,128)}, f32[2,512,512]{2,1,0:T(8,128)}, u32[]{:S(2)}, u32[]{:S(2)}) %collective-permute-start.3) | collective-permute-done | bytes 2097184 | tf_op jit(solution)/shard_map/ppermute | solution.py:111
  201.8 3.5 %fusion = bf16[2,512,512]{2,1,0:T(8,128)(2,1)} fusion(f32[2,512,512]{2,1,0:T(8,128)} %collective-permute-done.3, f32[2,2,512,512]{3,2,1,0:T(8,128)} %bitcast.56, s32[]{:T(128)S(6)} %select_n.44), kind=kLoop, calls=%fused_computation.6 | loop fusion | flops 1048576 | bytes 5242884 | tf_op jit(solution)/shard_map/convert_element_type | solution.py:114
  205.3 4.4 %all-to-all-start.2 = ((bf16[2,512,512]{2,1,0:T(8,128)(2,1)}), bf16[2,512,512]{2,1,0:T(8,128)(2,1)}, u32[]{:S(2)}, u32[]{:S(2)}) async-start(bf16[2,512,512]{2,1,0:T(8,128)(2,1)} %fusion), calls=%async_computation.2 | async-start | bytes 2097152 | tf_op jit(solution)/shard_map/all_to_all | solution.py:113
  209.8 3.1 %copy-done.4 = bf16[32,128,896]{2,1,0:T(8,128)(2,1)S(1)} copy-done((bf16[32,128,896]{2,1,0:T(8,128)(2,1)S(1)}, bf16[32,128,896]{2,1,0:T(8,128)(2,1)}, u32[]{:S(2)}) %copy-start.4) | copy-done | bytes 7340056
  212.8 8.9 %outer.1 = f32[896,512]{1,0:T(8,128)} custom-call(bf16[8,4,128,896]{3,2,1,0:T(8,128)(2,1)S(1)} %bitcast.58, bf16[4,8,144,64]{3,2,1,0:T(8,128)(2,1)S(1)} %multiply_convert_fusion.codes_ref, bf16[8,4,128,144]{3,2,1,0:T(8,128)(2,1)S(1)} %compare_convert_fusion.pick_ref), custom_call_target="tpu_custom_call" | custom-call | flops 3758096384 | bytes 7340032 | tf_op jit(solution)/shard_map/outer/pallas_call | solution.py:237
  221.7 2.3 all-to-all-done.2
  224.0 2.5 %convert_reduce_fusion = f32[512,512]{1,0:T(8,128)} fusion(bf16[2,512,512]{2,1,0:T(8,128)(2,1)} %all-to-all-done.2), kind=kLoop, calls=%fused_computation.7 | loop fusion | flops 786432 | bytes 2097152 | tf_op jit(solution)/shard_map/reduce_sum | solution.py:116
  (44 shorter events, 0.3 us)
Async XLA Ops:
  7.2 1.7 copy-start.8
  7.2 2.3 %copy-start.10 = (f32[3584]{0:T(1024)S(1)}, f32[3584]{0:T(1024)}, u32[]{:S(2)}) copy-start(f32[3584]{0:T(1024)} %param.16) | copy-start | bytes 43012
  7.2 3.6 %copy-start.13 = (s32[128]{0:T(128)S(1)}, s32[128]{0:T(128)}, u32[]{:S(2)}) copy-start(s32[128]{0:T(128)} %param.12) | copy-start | bytes 1540
  7.2 3.7 %copy-start.14 = (s32[128]{0:T(128)S(1)}, s32[128]{0:T(128)}, u32[]{:S(2)}) copy-start(s32[128]{0:T(128)} %param.13) | copy-start | bytes 1540
  7.2 139.1 %all-gather.4.cloned.1.call-start = ((), (), s32[]{:S(2)}) async-start(), calls=%async_computation.3 | async-start | bytes 8257536 | tf_op jit(solution)/shard_map/all_gather | solution.py:190
  12.5 18.6 %copy-start.6 = (bf16[512,512]{1,0:T(8,128)(2,1)S(1)}, bf16[512,512]{1,0:T(8,128)(2,1)}, u32[]{:S(2)}) copy-start(bf16[512,512]{1,0:T(8,128)(2,1)} %param.18) | copy-start | bytes 1572868
  12.5 19.7 %copy-start.11 = (s32[128,8]{0,1:T(8,128)S(1)}, s32[128,8]{0,1:T(8,128)}, u32[]{:S(2)}) copy-start(s32[128,8]{0,1:T(8,128)} %param.10) | copy-start | bytes 12292
  12.5 19.7 %copy-start.12 = (f32[128,8]{0,1:T(8,128)S(1)}, f32[128,8]{0,1:T(8,128)}, u32[]{:S(2)}) copy-start(f32[128,8]{0,1:T(8,128)} %param.11) | copy-start | bytes 12292
  31.0 84.8 %collective-permute-start = (bf16[512,512]{1,0:T(8,128)(2,1)S(1)}, bf16[512,512]{1,0:T(8,128)(2,1)S(1)}, u32[]{:S(2)}, u32[]{:S(2)}) collective-permute-start(bf16[512,512]{1,0:T(8,128)(2,1)S(1)} %copy-done.6), channel_id=1, source_target_pairs={{8,0},{16,8},{24,16},{0,24},{9,1},{17,9},{25,17},{1,25},{10,2},{18... | collective-permute-start | bytes 1572872 | tf_op jit(solution)/shard_map/ppermute | solution.py:123
  31.1 85.2 %collective-permute-start.1 = (bf16[512,512]{1,0:T(8,128)(2,1)S(1)}, bf16[512,512]{1,0:T(8,128)(2,1)}, u32[]{:S(2)}, u32[]{:S(2)}) collective-permute-start(bf16[512,512]{1,0:T(8,128)(2,1)S(1)} %copy-done.6), channel_id=1, source_target_pairs={{16,0},{24,8},{0,16},{8,24},{17,1},{25,9},{1,17},{9,25},{18,2},{26... | collective-permute-start | bytes 1572872 | tf_op jit(solution)/shard_map/ppermute | solution.py:123
  32.2 85.2 %collective-permute-start.2 = (bf16[512,512]{1,0:T(8,128)(2,1)S(1)}, bf16[512,512]{1,0:T(8,128)(2,1)}, u32[]{:S(2)}, u32[]{:S(2)}) collective-permute-start(bf16[512,512]{1,0:T(8,128)(2,1)S(1)} %copy-done.6), channel_id=1, source_target_pairs={{24,0},{0,8},{8,16},{16,24},{25,1},{1,9},{9,17},{17,25},{26,2},{2,... | collective-permute-start | bytes 1572872 | tf_op jit(solution)/shard_map/ppermute | solution.py:123
  112.9 3.4 %copy-start.7 = (bf16[3584,512]{1,0:T(8,128)(2,1)S(1)}, bf16[3584,512]{1,0:T(8,128)(2,1)}, u32[]{:S(2)}) copy-start(bf16[3584,512]{1,0:T(8,128)(2,1)} %constant_dynamic-update-slice_fusion.6) | copy-start | bytes 11010052
  130.0 11.0 %copy-start.9 = (f32[8,4,144,1]{2,0,1,3:T(8,128)S(1)}, f32[8,4,144,1]{2,0,1,3:T(8,128)}, u32[]{:S(2)}) copy-start(f32[8,4,144,1]{2,0,1,3:T(8,128)} %reshape.60) | copy-start | bytes 55300
  146.3 3.1 %copy-start.3 = (bf16[32,128,896]{2,1,0:T(8,128)(2,1)S(1)}, bf16[32,128,896]{2,1,0:T(8,128)(2,1)}, u32[]{:S(2)}) copy-start(bf16[32,128,896]{2,1,0:T(8,128)(2,1)} %all-gather.4.cloned.1.call-done) | copy-start | bytes 22020100
  149.4 1.2 copy-start.5
  160.2 1.0 copy-start.2
  161.2 20.2 %all-to-all-start.1 = ((f32[4,8,72,128]{3,2,1,0:T(8,128)}), f32[4,8,72,128]{3,2,1,0:T(8,128)}, u32[]{:S(2)}, u32[]{:S(2)}) async-start(f32[4,8,72,128]{3,2,1,0:T(8,128)} %copy-done.2), calls=%async_computation.1 | async-start | bytes 2359296 | tf_op jit(solution)/shard_map/all_to_all | solution.py:226
  187.3 2.3 %copy-start = (bf16[8,144,2048]{2,1,0:T(8,128)(2,1)S(1)}, bf16[8,144,2048]{2,1,0:T(8,128)(2,1)}, u32[]{:S(2)}) copy-start(bf16[8,144,2048]{2,1,0:T(8,128)(2,1)} %hidden_ref.1) | copy-start | bytes 14155780
  193.7 2.1 copy-start.1
  197.3 4.5 %collective-permute-start.3 = (f32[2,512,512]{2,1,0:T(8,128)}, f32[2,512,512]{2,1,0:T(8,128)}, u32[]{:S(2)}, u32[]{:S(2)}) collective-permute-start(f32[2,512,512]{2,1,0:T(8,128)} %dynamic-slice_bitcast_fusion), channel_id=1, source_target_pairs={{0,8},{8,0},{16,24},{24,16},{1,9},{9,1},{17,25},{25,17},{2,10},{10... | collective-permute-start | bytes 6291464 | tf_op jit(solution)/shard_map/ppermute | solution.py:111
  205.3 18.7 %all-to-all-start.2 = ((bf16[2,512,512]{2,1,0:T(8,128)(2,1)}), bf16[2,512,512]{2,1,0:T(8,128)(2,1)}, u32[]{:S(2)}, u32[]{:S(2)}) async-start(bf16[2,512,512]{2,1,0:T(8,128)(2,1)} %fusion), calls=%async_computation.2 | async-start | bytes 2097152 | tf_op jit(solution)/shard_map/all_to_all | solution.py:113
  209.7 3.1 %copy-start.4 = (bf16[32,128,896]{2,1,0:T(8,128)(2,1)S(1)}, bf16[32,128,896]{2,1,0:T(8,128)(2,1)}, u32[]{:S(2)}) copy-start(bf16[32,128,896]{2,1,0:T(8,128)(2,1)} %all-gather.4.cloned.1.call-done) | copy-start | bytes 22020100
Sparse Core Ops, SparseCore 0:
  31.2 115.0 all-gather.3
